TPU v7x, 256 devices: a whole 4x4x8 slice. The times are simulated.
256 devices in a mesh: blocks: 64 (over z, y, core), views: 4 (over x).
Axes of the slice: x: 4, y: 4, z: 8, core: 2. Of those that a mesh axis runs over, the one named last changes fastest.
Arguments:
- params: float32 [59, 131072], P(None, 'blocks'), as said below
- moment1: float32 [59, 131072], P(None, 'blocks'), may hold values from -0.046875 to 0.046875
- moment2: float32 [59, 131072], P(None, 'blocks'), may hold values from 1e-09 to 0.001
- dual: float32 [59, 65536], P(None, 'blocks'), may hold values from -4 to 4
- z_copy: float32 [59, 65536], P(None, 'blocks'), may hold values from -6 to 6
- z_table: float32 [59, 65536], P(None, 'blocks'), may hold values from -6 to 6
- boundary_rows: int32 [65536], P('blocks'), may hold values from 0 to 2047
- owner_block: int32 [65536, 1], P('blocks'), may hold values from 0 to 63; in each aligned block of 1024 rows (0 to 1023, 1024 to 2047, ...) at most 64 rows name the same one
- owner_slot: int32 [65536], P('blocks'), may hold values from 0 to 1023
- tile_lists: int32 [4096, 32], P(('blocks', 'views')), may hold values from 0 to 2047
- tile_counts: int32 [4096], P(('blocks', 'views')), may hold values from 8 to 32, as said below
- cameras: float32 [256, 24], P(('blocks', 'views'))
- target: float32 [3, 1048576], P(None, ('blocks', 'views')), may hold values from 0 to 1
Outputs:
- new_params: float32 [59, 131072], P(None, 'blocks')
- new_moment1: float32 [59, 131072], P(None, 'blocks')
- new_moment2: float32 [59, 131072], P(None, 'blocks')
- z_new: float32 [59, 65536], P(None, 'blocks')
- dual_new: float32 [59, 65536], P(None, 'blocks')
Inputs may be any that keep to these rules, and one draw needn't show every extreme that they name: `tile_lists`: rows of the Gaussian lists from slot tile_counts on are padding. `tile_counts`: every device has a tile with all 32 slots live. `owner_block`: among the 1024 copies of one block at most 64 name the same owner, and some owner gets exactly 64. `params`: the quaternion's first entry is 1 or more.
All inputs are finite; a program needn't handle non-finite values.
Results may differ from a plain program's by a relative error of at most 0.0003.
Values sent between devices are 32-bit elements; how exact they have to be, the bound alone decides.
A program may use at most 64 MiB of HBM per device.

v0:
```python
import functools

import jax
import jax.numpy as jnp
from jax import lax
from jax.experimental import pallas as pl
from jax.experimental.pallas import tpu as pltpu
from jax.sharding import PartitionSpec as P

LEARN = 0.05
BETA_ONE = 0.9
BETA_TWO = 0.999
EPSILON = 1e-08

NPAR = 59
GAUSS = 2048
COPIES = 1024
ROWS = 1024
TILES = 16
DEPTH = 32
PAIRS = TILES * DEPTH
PIXELS = 256
NBLK = 64
NVIEW = 4
CAP = 64
SHARE = 15
WIDE = PAIRS + 128
JOINT = NVIEW * PAIRS + COPIES

F32 = jnp.float32
BF16 = jnp.bfloat16
I32 = jnp.int32
MESH = pl.DeviceIdType.MESH
NT = (((1,), (1,)), ((), ()))


def lane_gather(source, index, groups):
    low = index & 127
    high = index >> 7
    found = [jnp.take_along_axis(part, low, axis=1) for part in source[0]]
    for g in range(1, groups):
        here = high == g
        for n, part in enumerate(source[g]):
            found[n] = jnp.where(here, jnp.take_along_axis(part, low, axis=1), found[n])
    return found


def wide(row):
    return jnp.broadcast_to(row, (8, row.shape[1]))


def split(value):
    high = value.astype(BF16)
    return high, (value - high.astype(F32)).astype(BF16)


def share_of(ref, view):
    parts = [ref[SHARE * v : SHARE * v + 16, :] for v in range(NVIEW)]
    result = parts[3]
    for v in range(3):
        result = jnp.where(view == v, parts[v], result)
    return result


def render_kernel(cam, params, listed, target, out, table, sheet, goal, e_all, t_all, parts):
    table[0:11, :] = params[0:11, :]
    table[14:16, :] = jnp.zeros((2, GAUSS), F32)
    for c in range(3):
        colour = cam[0, 8] * params[11 + 16 * c : 12 + 16 * c, :]
        for k in range(1, 16):
            row = 11 + 16 * c + k
            colour += cam[0, 8 + k] * params[row : row + 1, :]
        table[11 + c : 12 + c, :] = colour + 0.5
    for c in range(3):
        for t in range(TILES):
            goal[16 * c + t : 16 * c + t + 1, :] = target[c : c + 1, PIXELS * t : PIXELS * (t + 1)]

    coded = listed[...]
    live = jnp.where(coded < GAUSS, 1.0, 0.0)
    index = coded & (GAUSS - 1)
    picked = []
    for j in range(PAIRS // 128):
        lanes = wide(index[:, 128 * j : 128 * (j + 1)])
        source = [
            [table[8 * n : 8 * n + 8, 128 * g : 128 * (g + 1)] for n in range(2)]
            for g in range(GAUSS // 128)
        ]
        picked.append(jnp.concatenate(lane_gather(source, lanes, GAUSS // 128), axis=0))
    picked = jnp.concatenate(picked, axis=1)

    def take(row):
        return picked[row : row + 1, :]

    jac = [[cam[0, 3 * i + j] for j in range(3)] for i in range(2)]
    centre = [take(j) for j in range(3)]
    scale = [jnp.exp(take(3 + k)) for k in range(3)]
    quat = [take(6 + k) for k in range(4)]
    norm = 1.0 / jnp.sqrt(quat[0] * quat[0] + quat[1] * quat[1] + quat[2] * quat[2] + quat[3] * quat[3])
    qw, qx, qy, qz = [q * norm for q in quat]
    rot = [
        [1 - 2 * (qy * qy + qz * qz), 2 * (qx * qy - qw * qz), 2 * (qx * qz + qw * qy)],
        [2 * (qx * qy + qw * qz), 1 - 2 * (qx * qx + qz * qz), 2 * (qy * qz - qw * qx)],
        [2 * (qx * qz - qw * qy), 2 * (qy * qz + qw * qx), 1 - 2 * (qx * qx + qy * qy)],
    ]
    mixed = [
        [(jac[i][0] * rot[0][k] + jac[i][1] * rot[1][k] + jac[i][2] * rot[2][k]) * scale[k] for k in range(3)]
        for i in range(2)
    ]

    def inner(a, b):
        return a[0] * b[0] + a[1] * b[1] + a[2] * b[2]

    first = inner(mixed[0], mixed[0]) + 0.01
    second = inner(mixed[1], mixed[1]) + 0.01
    cross = inner(mixed[0], mixed[1])
    det = first * second - cross * cross
    con0, con1, con2 = second / det, -cross / det, first / det
    cu = inner(jac[0], centre) + cam[0, 6]
    cw = inner(jac[1], centre) + cam[0, 7]
    opacity = 1.0 / (1.0 + jnp.exp(-take(10)))
    shown = opacity * live

    rows = [cu, cw, con0, 2.0 * con1, con2, shown, take(11), take(12), take(13)]
    rows = jnp.concatenate(rows + [jnp.zeros((7, PAIRS), F32)], axis=0)
    sheet[...] = rows.T

    tile = lax.broadcasted_iota(I32, (TILES, PIXELS), 0)
    pixel = lax.broadcasted_iota(I32, (TILES, PIXELS), 1)
    pos_u = (((tile & 3) * 16 + (pixel & 15)).astype(F32) + 0.5) / 32.0 - 1.0
    pos_w = (((tile >> 2) * 16 + (pixel >> 4)).astype(F32) + 0.5) / 32.0 - 1.0

    def column(s, f):
        return jnp.broadcast_to(sheet[16 * s : 16 * s + 16, f : f + 1], (TILES, PIXELS))

    image = [jnp.zeros((TILES, PIXELS), F32)] * 3
    passed = jnp.ones((TILES, PIXELS), F32)
    for s in range(DEPTH):
        du = pos_u - column(s, 0)
        dw = pos_w - column(s, 1)
        quad = (column(s, 2) * du + column(s, 3) * dw) * du + column(s, 4) * dw * dw
        bell = jnp.exp(-0.5 * quad)
        alpha = jnp.minimum(column(s, 5) * bell, 0.99)
        weight = alpha * passed
        for c in range(3):
            image[c] = image[c] + column(s, 6 + c) * weight
        e_all[16 * s : 16 * s + 16, :] = bell
        t_all[16 * s : 16 * s + 16, :] = passed
        passed = passed - weight

    diff = [image[c] - goal[16 * c : 16 * c + 16, :] for c in range(3)]
    behind = jnp.zeros((TILES, PIXELS), F32)
    for s in range(DEPTH - 1, -1, -1):
        bell = e_all[16 * s : 16 * s + 16, :]
        before = t_all[16 * s : 16 * s + 16, :]
        raw = column(s, 5) * bell
        alpha = jnp.minimum(raw, 0.99)
        glow = diff[0] * column(s, 6) + diff[1] * column(s, 7) + diff[2] * column(s, 8)
        slope = before * (glow - behind)
        slope = jnp.where(raw < 0.99, slope, jnp.where(raw == 0.99, 0.5 * slope, 0.0))
        behind = behind + alpha * (glow - behind)
        weight = alpha * before
        sums = [-0.5 * raw * slope, bell * slope] + [diff[c] * weight for c in range(3)]
        for n, value in enumerate(sums):
            high, low = split(value)
            parts[2 * n, 16 * s : 16 * s + 16, :] = high
            parts[2 * n + 1, 16 * s : 16 * s + 16, :] = low

    which = lax.broadcasted_iota(I32, (16, PIXELS), 0)
    place = lax.broadcasted_iota(I32, (16, PIXELS), 1)
    in_u = ((place & 15).astype(F32) - 7.5) / 32.0
    in_w = ((place >> 4).astype(F32) - 7.5) / 32.0
    basis = jnp.where(which == 0, 1.0, 0.0)
    basis = jnp.where(which == 1, in_u, basis)
    basis = jnp.where(which == 2, in_w, basis)
    basis = jnp.where(which == 3, in_u * in_u, basis)
    basis = jnp.where(which == 4, in_u * in_w, basis)
    basis = jnp.where(which == 5, in_w * in_w, basis)
    basis = basis.astype(BF16)

    def over_pixels(n):
        return lax.dot_general(basis, parts[2 * n], NT, preferred_element_type=F32) + lax.dot_general(
            basis, parts[2 * n + 1], NT, preferred_element_type=F32
        )

    moments = over_pixels(0)
    m1, mu, mw, muu, muw, mww = [moments[n : n + 1, :] for n in range(6)]
    g_opacity = over_pixels(1)[0:1, :] * live
    g_colour = [over_pixels(2 + c)[0:1, :] for c in range(3)]
    at = lax.broadcasted_iota(I32, (1, PAIRS), 1) & 15
    off_u = cu - (((at & 3) * 16 + 8).astype(F32) / 32.0 - 1.0)
    off_w = cw - (((at >> 2) * 16 + 8).astype(F32) / 32.0 - 1.0)
    s_u = mu - off_u * m1
    s_w = mw - off_w * m1
    g_con0 = muu - off_u * (mu + s_u)
    g_con1 = 2.0 * (muw - off_u * mw - off_w * s_u)
    g_con2 = mww - off_w * (mw + s_w)
    g_cu = -2.0 * (con0 * s_u + con1 * s_w)
    g_cw = -2.0 * (con1 * s_u + con2 * s_w)

    g_first = -(con0 * con0 * g_con0 + con0 * con1 * g_con1 + con1 * con1 * g_con2)
    g_second = -(con1 * con1 * g_con0 + con1 * con2 * g_con1 + con2 * con2 * g_con2)
    g_cross = -(2.0 * con0 * con1 * g_con0 + (con0 * con2 + con1 * con1) * g_con1 + 2.0 * con1 * con2 * g_con2)
    g_mixed = [
        [2.0 * g_first * mixed[0][k] + g_cross * mixed[1][k] for k in range(3)],
        [2.0 * g_second * mixed[1][k] + g_cross * mixed[0][k] for k in range(3)],
    ]
    g_scale = [g_mixed[0][k] * mixed[0][k] + g_mixed[1][k] * mixed[1][k] for k in range(3)]
    r = [
        [(jac[0][j] * g_mixed[0][k] + jac[1][j] * g_mixed[1][k]) * scale[k] for k in range(3)] for j in range(3)
    ]
    h_w = 2 * (qz * (r[1][0] - r[0][1]) + qy * (r[0][2] - r[2][0]) + qx * (r[2][1] - r[1][2]))
    h_x = 2 * (
        qy * (r[0][1] + r[1][0]) + qz * (r[0][2] + r[2][0]) + qw * (r[2][1] - r[1][2]) - 2 * qx * (r[1][1] + r[2][2])
    )
    h_y = 2 * (
        qx * (r[0][1] + r[1][0]) + qz * (r[1][2] + r[2][1]) + qw * (r[0][2] - r[2][0]) - 2 * qy * (r[0][0] + r[2][2])
    )
    h_z = 2 * (
        qx * (r[0][2] + r[2][0]) + qy * (r[1][2] + r[2][1]) + qw * (r[1][0] - r[0][1]) - 2 * qz * (r[0][0] + r[1][1])
    )
    along = qw * h_w + qx * h_x + qy * h_y + qz * h_z
    g_quat = [(h - q * along) * norm for h, q in ((h_w, qw), (h_x, qx), (h_y, qy), (h_z, qz))]
    g_centre = [jac[0][j] * g_cu + jac[1][j] * g_cw for j in range(3)]
    g_logit = g_opacity * opacity * (1.0 - opacity)
    sent = g_centre + g_scale + g_quat + [g_logit] + g_colour + [index.astype(F32), jnp.zeros((1, PAIRS), F32)]
    out[:, 0:PAIRS] = jnp.concatenate(sent, axis=0)
    spot = lax.broadcasted_iota(I32, (16, 128), 0)
    colbasis = jnp.zeros((16, 128), F32)
    for k in range(16):
        colbasis = jnp.where(spot == k, cam[0, 8 + k], colbasis)
    out[:, PAIRS:WIDE] = colbasis


def views_kernel(mine, out, send_sem, recv_sem):
    view = lax.axis_index("views")
    barrier = pltpu.get_barrier_semaphore()
    for k in range(1, NVIEW):
        pl.semaphore_signal(barrier, inc=1, device_id={"views": (view + k) % NVIEW}, device_id_type=MESH)
    pl.semaphore_wait(barrier, NVIEW - 1)
    copies = []
    for k in range(1, NVIEW):
        copy = pltpu.make_async_remote_copy(
            src_ref=mine,
            dst_ref=out.at[view],
            send_sem=send_sem.at[k - 1],
            recv_sem=recv_sem.at[k - 1],
            device_id={"views": (view + k) % NVIEW},
            device_id_type=MESH,
        )
        copy.start()
        copies.append(copy)
    out[view] = mine[...]
    for copy in copies:
        copy.wait()


def update_kernel(
    gathered, params, moment1, moment2, dual, z_copy, rows, owner, slot,
    new_params, new_moment1, new_moment2, send, holds, place,
    left, masked, onehot, padded, padded_dual, source, names,
):
    view = lax.axis_index("views")
    left[59:64, :] = jnp.zeros((5, JOINT), F32)
    for v in range(NVIEW):
        lanes = slice(PAIRS * v, PAIRS * (v + 1))
        left[0:11, lanes] = gathered[v, 0:11, 0:PAIRS]
        colbasis = gathered[v, :, PAIRS : PAIRS + 1]
        for c in range(3):
            left[11 + 16 * c : 27 + 16 * c, lanes] = colbasis * gathered[v, 11 + c : 12 + c, 0:PAIRS]
    lanes = slice(NVIEW * PAIRS, JOINT)
    left[0:NPAR, lanes] = dual[...] - z_copy[...]
    left[NPAR : NPAR + 1, lanes] = jnp.ones((1, COPIES), F32)
    boundary = rows[...]
    joint = jnp.concatenate([gathered[v, 14:15, 0:PAIRS].astype(I32) for v in range(NVIEW)] + [boundary], axis=1)
    high, low = split(left[...])
    group = joint >> 8
    for h in range(8):
        mask = jnp.where(jnp.broadcast_to(group, (16, JOINT)) == h, 1.0, 0.0).astype(BF16)
        for n in range(4):
            masked[128 * h + 16 * n : 128 * h + 16 * n + 16, :] = high[16 * n : 16 * n + 16, :] * mask
            masked[128 * h + 64 + 16 * n : 128 * h + 80 + 16 * n, :] = low[16 * n : 16 * n + 16, :] * mask
    inside = joint & 255
    hot = lax.broadcasted_iota(I32, (256, JOINT), 0) == inside
    onehot[...] = jnp.where(hot, 1.0, 0.0).astype(BF16)
    total = lax.dot_general(masked[...], onehot[...], NT, preferred_element_type=F32)

    padded[NPAR:64, :] = jnp.zeros((64 - NPAR, GAUSS), F32)
    for h in range(8):
        both = total[128 * h : 128 * h + 64, :] + total[128 * h + 64 : 128 * h + 128, :]
        lanes = slice(256 * h, 256 * (h + 1))
        value = params[:, lanes]
        grad = both[0:NPAR] + both[NPAR : NPAR + 1] * value
        first = BETA_ONE * moment1[:, lanes] + (1.0 - BETA_ONE) * grad
        second = BETA_TWO * moment2[:, lanes] + (1.0 - BETA_TWO) * grad * grad
        mhat = first * (1.0 / (1.0 - BETA_ONE**10))
        vhat = second * (1.0 / (1.0 - BETA_TWO**10))
        value = value - LEARN * mhat / (jnp.sqrt(vhat) + EPSILON)
        new_moment1[:, lanes] = first
        new_moment2[:, lanes] = second
        new_params[:, lanes] = value
        padded[0:NPAR, lanes] = value
    padded_dual[0:NPAR, :] = dual[...]
    padded_dual[NPAR:64, :] = jnp.zeros((64 - NPAR, COPIES), F32)

    owned = lax.broadcasted_iota(I32, (NBLK, COPIES), 0) == owner[...]
    owned = jnp.where(owned, 1.0, 0.0)
    upper = lax.broadcasted_iota(I32, (128, 128), 0) < lax.broadcasted_iota(I32, (128, 128), 1)
    upper = jnp.where(upper, 1.0, 0.0).astype(BF16)
    ranks = []
    carry = jnp.zeros((NBLK, 1), F32)
    for j in range(COPIES // 128):
        part = owned[:, 128 * j : 128 * (j + 1)]
        ahead = jnp.dot(part.astype(BF16), upper, preferred_element_type=F32) + carry
        ranks.append(jnp.sum(part * ahead, axis=0, keepdims=True))
        carry = carry + jnp.sum(part, axis=1, keepdims=True)
    rank = jnp.concatenate(ranks, axis=1).astype(I32)
    place[...] = owner[...] * CAP + rank
    ident = lax.broadcasted_iota(I32, (1, COPIES), 1)
    ranked = (lax.broadcasted_iota(I32, (128, COPIES), 0) & (CAP - 1)) == rank
    coarse = jnp.where(ranked, (ident >> 5).astype(F32), 0.0).astype(BF16)
    fine = jnp.where(ranked, ((ident & 31) + 1).astype(F32), 0.0).astype(BF16)
    owned = owned.astype(BF16)
    names[...] = (
        32.0 * lax.dot_general(owned, coarse, NT, preferred_element_type=F32)
        + lax.dot_general(owned, fine, NT, preferred_element_type=F32)
    ).astype(I32)

    mine = share_of(padded, view)
    xs = []
    for j in range(COPIES // 128):
        parts = [
            [mine[8 * n : 8 * n + 8, 128 * g : 128 * (g + 1)] for n in range(2)] for g in range(GAUSS // 128)
        ]
        xs.append(jnp.concatenate(lane_gather(parts, wide(boundary[:, 128 * j : 128 * (j + 1)]), GAUSS // 128), axis=0))
    source[...] = jnp.concatenate(xs, axis=1) + share_of(padded_dual, view)
    source[15:16, :] = (slot[...] + 1).astype(F32)
    holds[...] = source[...]

    lane = lax.broadcasted_iota(I32, (8, 128), 1)
    for j in range(NBLK // 2):
        name = jnp.where(lane < CAP, wide(names[2 * j : 2 * j + 1, :]), wide(names[2 * j + 1 : 2 * j + 2, :]))
        parts = [
            [source[8 * n : 8 * n + 8, 128 * g : 128 * (g + 1)] for n in range(2)] for g in range(COPIES // 128)
        ]
        top, bottom = lane_gather(parts, jnp.maximum(name - 1, 0), COPIES // 128)
        top = jnp.where(name > 0, top, 0.0)
        bottom = jnp.where(name > 0, bottom, 0.0)
        send[2 * j] = jnp.where(lane < CAP, top, pltpu.roll(bottom, CAP, 1))
        send[2 * j + 1] = jnp.where(lane < CAP, pltpu.roll(top, CAP, 1), bottom)


def to_blocks(outgoing, incoming, send_sem, recv_sem, block):
    def one(k, _):
        other = (block + k) % NBLK
        pltpu.make_async_remote_copy(
            src_ref=outgoing.at[other],
            dst_ref=incoming.at[block],
            send_sem=send_sem,
            recv_sem=recv_sem,
            device_id={"blocks": other},
            device_id_type=MESH,
        ).start()
        return 0

    lax.fori_loop(1, NBLK, one, 0)
    incoming[block] = outgoing[block]


def wait_blocks(outgoing, incoming, send_sem, recv_sem, block):
    whole = pltpu.make_async_remote_copy(
        src_ref=outgoing.at[pl.ds(0, NBLK - 1)],
        dst_ref=incoming.at[pl.ds(0, NBLK - 1)],
        send_sem=send_sem,
        recv_sem=recv_sem,
        device_id={"blocks": block},
        device_id_type=MESH,
    )
    whole.wait_send()
    whole.wait_recv()


def to_views(pieces, send_sem, recv_sem, view):
    copies = []
    for k in range(1, NVIEW):
        copy = pltpu.make_async_remote_copy(
            src_ref=pieces.at[view],
            dst_ref=pieces.at[view],
            send_sem=send_sem.at[k - 1],
            recv_sem=recv_sem.at[k - 1],
            device_id={"views": (view + k) % NVIEW},
            device_id_type=MESH,
        )
        copy.start()
        copies.append(copy)
    return copies


def unpack(chunks, j):
    lane = lax.broadcasted_iota(I32, (8, 128), 1)
    even, odd = chunks[2 * j], chunks[2 * j + 1]
    top = jnp.where(lane < CAP, even, pltpu.roll(odd, CAP, 1))
    bottom = jnp.where(lane < CAP, pltpu.roll(even, CAP, 1), odd)
    return top, bottom


def consensus_kernel(
    send, z_table, holds, place,
    z_new, dual_new,
    got, answers, returned, z_parts, d_parts, padded, items, masked, onehot,
    s_send, r_send, s_back, r_back, s_z, r_z, s_d, r_d,
):
    block = lax.axis_index("blocks")
    view = lax.axis_index("views")
    barrier = pltpu.get_barrier_semaphore()

    def greet(k, _):
        pl.semaphore_signal(barrier, inc=1, device_id={"blocks": (block + k) % NBLK}, device_id_type=MESH)
        return 0

    lax.fori_loop(1, NBLK, greet, 0)
    for k in range(1, NVIEW):
        pl.semaphore_signal(barrier, inc=1, device_id={"views": (view + k) % NVIEW}, device_id_type=MESH)
    pl.semaphore_wait(barrier, NBLK - 1 + NVIEW - 1)
    to_blocks(send, got, s_send, r_send, block)
    padded[0:NPAR, :] = z_table[...]
    padded[NPAR:64, :] = jnp.zeros((64 - NPAR, ROWS), F32)
    wait_blocks(send, got, s_send, r_send, block)

    for j in range(NBLK // 2):
        top, bottom = unpack(got, j)
        items[0:8, 128 * j : 128 * (j + 1)] = top
        items[8:16, 128 * j : 128 * (j + 1)] = bottom
    label = items[15:16, :].astype(I32)
    index = jnp.maximum(label - 1, 0)
    present = label > 0
    last = lax.broadcasted_iota(I32, (16, NBLK * CAP), 0) == 15
    high, low = split(jnp.where(last, 1.0, items[...]))
    group = jnp.where(present, index >> 8, 4)
    for h in range(4):
        mask = jnp.where(jnp.broadcast_to(group, (16, NBLK * CAP)) == h, 1.0, 0.0).astype(BF16)
        masked[32 * h : 32 * h + 16, :] = high * mask
        masked[32 * h + 16 : 32 * h + 32, :] = low * mask
    hot = lax.broadcasted_iota(I32, (256, NBLK * CAP), 0) == (index & 255)
    onehot[...] = jnp.where(hot, 1.0, 0.0).astype(BF16)
    total = lax.dot_general(masked[...], onehot[...], NT, preferred_element_type=F32)
    mine = share_of(padded, view)
    fresh = []
    for h in range(4):
        both = total[32 * h : 32 * h + 16, :] + total[32 * h + 16 : 32 * h + 32, :]
        fresh.append((mine[:, 256 * h : 256 * (h + 1)] + both) / (1.0 + both[15:16, :]))
    fresh = jnp.concatenate(fresh, axis=1)
    z_parts[view] = fresh
    z_copies = to_views(z_parts, s_z, r_z, view)

    lane = lax.broadcasted_iota(I32, (8, 128), 1)
    parts = [[fresh[8 * n : 8 * n + 8, 128 * g : 128 * (g + 1)] for n in range(2)] for g in range(ROWS // 128)]
    for j in range(NBLK // 2):
        top, bottom = lane_gather(parts, wide(index[:, 128 * j : 128 * (j + 1)]), ROWS // 128)
        answers[2 * j] = jnp.where(lane < CAP, top, pltpu.roll(bottom, CAP, 1))
        answers[2 * j + 1] = jnp.where(lane < CAP, pltpu.roll(top, CAP, 1), bottom)
    to_blocks(answers, returned, s_back, r_back, block)
    wait_blocks(answers, returned, s_back, r_back, block)

    for j in range(NBLK // 2):
        top, bottom = unpack(returned, j)
        items[0:8, 128 * j : 128 * (j + 1)] = top
        items[8:16, 128 * j : 128 * (j + 1)] = bottom
    fetched = []
    for j in range(COPIES // 128):
        parts = [
            [items[8 * n : 8 * n + 8, 128 * g : 128 * (g + 1)] for n in range(2)] for g in range(NBLK // 2)
        ]
        fetched.append(
            jnp.concatenate(lane_gather(parts, wide(place[:, 128 * j : 128 * (j + 1)]), NBLK // 2), axis=0)
        )
    d_parts[view] = holds[...] - jnp.concatenate(fetched, axis=1)
    d_copies = to_views(d_parts, s_d, r_d, view)
    for copy in z_copies:
        copy.wait()
    for v in range(NVIEW):
        count = min(SHARE, NPAR - SHARE * v)
        z_new[SHARE * v : SHARE * v + count, :] = z_parts[v, 0:count, :]
    for copy in d_copies:
        copy.wait()
    for v in range(NVIEW):
        count = min(SHARE, NPAR - SHARE * v)
        dual_new[SHARE * v : SHARE * v + count, :] = d_parts[v, 0:count, :]


def vmem():
    return pl.BlockSpec(memory_space=pltpu.VMEM)


def local(
    params, moment1, moment2, dual, z_copy, z_table, boundary_rows, owner_block, owner_slot,
    tile_lists, tile_counts, cameras, target,
):
    spots = jnp.arange(DEPTH, dtype=I32)[None, :]
    listed = jnp.where(spots < tile_counts[:, None], tile_lists, tile_lists + GAUSS).T.reshape(1, PAIRS)
    limit = 48 * 1024 * 1024
    shape = jax.ShapeDtypeStruct
    mine = pl.pallas_call(
        render_kernel,
        out_shape=shape((16, WIDE), F32),
        in_specs=[pl.BlockSpec(memory_space=pltpu.SMEM), vmem(), vmem(), vmem()],
        out_specs=vmem(),
        scratch_shapes=[
            pltpu.VMEM((16, GAUSS), F32),
            pltpu.VMEM((PAIRS, 16), F32),
            pltpu.VMEM((48, PIXELS), F32),
            pltpu.VMEM((PAIRS, PIXELS), F32),
            pltpu.VMEM((PAIRS, PIXELS), F32),
            pltpu.VMEM((10, PAIRS, PIXELS), BF16),
        ],
        compiler_params=pltpu.CompilerParams(vmem_limit_bytes=limit),
        name="render",
    )(cameras, params, listed, target)
    gathered = pl.pallas_call(
        views_kernel,
        out_shape=shape((NVIEW, 16, WIDE), F32),
        in_specs=[vmem()],
        out_specs=vmem(),
        scratch_shapes=[pltpu.SemaphoreType.DMA((3,)), pltpu.SemaphoreType.DMA((3,))],
        compiler_params=pltpu.CompilerParams(collective_id=0, has_side_effects=True),
        name="exchange_views",
    )(mine)
    new_params, new_moment1, new_moment2, send, holds, place = pl.pallas_call(
        update_kernel,
        out_shape=(
            shape((NPAR, GAUSS), F32),
            shape((NPAR, GAUSS), F32),
            shape((NPAR, GAUSS), F32),
            shape((NBLK, 8, 128), F32),
            shape((16, COPIES), F32),
            shape((1, COPIES), I32),
        ),
        in_specs=[vmem()] * 9,
        out_specs=(vmem(),) * 6,
        scratch_shapes=[
            pltpu.VMEM((64, JOINT), F32),
            pltpu.VMEM((1024, JOINT), BF16),
            pltpu.VMEM((256, JOINT), BF16),
            pltpu.VMEM((64, GAUSS), F32),
            pltpu.VMEM((64, COPIES), F32),
            pltpu.VMEM((16, COPIES), F32),
            pltpu.VMEM((NBLK, 128), I32),
        ],
        compiler_params=pltpu.CompilerParams(vmem_limit_bytes=limit),
        name="update",
    )(
        gathered, params, moment1, moment2, dual, z_copy,
        boundary_rows.reshape(1, COPIES), owner_block.reshape(1, COPIES), owner_slot.reshape(1, COPIES),
    )
    z_new, dual_new = pl.pallas_call(
        consensus_kernel,
        out_shape=(shape((NPAR, ROWS), F32), shape((NPAR, COPIES), F32)),
        in_specs=[vmem()] * 4,
        out_specs=(vmem(),) * 2,
        scratch_shapes=[
            pltpu.VMEM((NBLK, 8, 128), F32),
            pltpu.VMEM((NBLK, 8, 128), F32),
            pltpu.VMEM((NBLK, 8, 128), F32),
            pltpu.VMEM((NVIEW, 16, ROWS), F32),
            pltpu.VMEM((NVIEW, 16, COPIES), F32),
            pltpu.VMEM((64, ROWS), F32),
            pltpu.VMEM((16, NBLK * CAP), F32),
            pltpu.VMEM((128, NBLK * CAP), BF16),
            pltpu.VMEM((256, NBLK * CAP), BF16),
            pltpu.SemaphoreType.DMA,
            pltpu.SemaphoreType.DMA,
            pltpu.SemaphoreType.DMA,
            pltpu.SemaphoreType.DMA,
            pltpu.SemaphoreType.DMA((3,)),
            pltpu.SemaphoreType.DMA((3,)),
            pltpu.SemaphoreType.DMA((3,)),
            pltpu.SemaphoreType.DMA((3,)),
        ],
        compiler_params=pltpu.CompilerParams(collective_id=1, has_side_effects=True, vmem_limit_bytes=limit),
        name="consensus",
    )(send, z_table, holds, place)
    return (new_params, new_moment1, new_moment2, z_new, dual_new)


def solution(mesh):
    whole, both = P(None, "blocks"), ("blocks", "views")
    placed = (whole,) * 6 + (P("blocks"), P("blocks", None), P("blocks"))
    placed += (P(both, None), P(both), P(both, None), P(None, both))
    return jax.shard_map(local, mesh=mesh, in_specs=placed, out_specs=(whole,) * 5, check_vma=False)
```

profile of v0, /device:TPU:1, one launch (start us, length us, event | category | flops | bytes accessed | tf_op | source)
XLA Modules:
  0.0 64.4 jit_solution(15955313079765694565)
XLA Ops:
  0.6 0.0 copy-start.9
  0.6 0.8 %fusion = s32[32,16]{0,1:T(8,128)S(1)} fusion(s32[16,32]{1,0:T(8,128)} %param.22, s32[16]{0:T(128)} %param.23), kind=kLoop, calls=%fused_computation.1 | loop fusion | flops 1536 | bytes 4160 | tf_op jit(solution)/shard_map/transpose | solution.py:499
  1.4 0.1 copy.19
  1.5 0.1 reshape.23.listed
  1.6 0.0 copy-done.9
  1.6 0.0 copy-start
  1.6 1.0 %copy-done = f32[59,2048]{1,0:T(8,128)S(1)} copy-done((f32[59,2048]{1,0:T(8,128)S(1)}, f32[59,2048]{1,0:T(8,128)}, u32[]{:S(2)}) %copy-start) | copy-done | bytes 483352
  2.7 0.0 copy-start.13
  2.7 0.7 %copy-done.13 = f32[1,24]{1,0:T(1,128)S(1)} copy-done((f32[1,24]{1,0:T(1,128)S(1)}, f32[1,24]{1,0:T(1,128)}, u32[]{:S(2)}) %copy-start.13) | copy-done | bytes 120
  3.3 0.0 copy-start.1
  3.3 0.0 copy-start.5
  3.3 3.4 %render.1.mine = f32[16,640]{1,0:T(8,128)S(1)} custom-call(f32[1,24]{1,0:T(1,128)S(1)} %copy-done.13, f32[59,2048]{1,0:T(8,128)S(1)} %copy-done, s32[1,512]{1,0:T(1,128)S(1)} %reshape.23.listed, f32[3,4096]{1,0:T(4,128)S(1)} %copy-done.9), custom_call_target="tpu_custom_call" | custom-call | tf_op jit(solution)/shard_map/render/pallas_call | solution.py:502
  6.7 0.0 copy-start.8
  6.7 0.6 copy-done.8
  7.4 0.0 copy-start.10
  7.4 0.0 copy-start.11
  7.4 0.0 copy-start.12
  7.4 7.9 %exchange_views.1.gathered = f32[4,16,640]{2,1,0:T(8,128)} custom-call(f32[16,640]{1,0:T(8,128)} %copy-done.8), custom_call_target="tpu_custom_call" | custom-call | tf_op jit(solution)/shard_map/exchange_views/pallas_call | solution.py:518
  15.2 0.0 copy-done.1
  15.3 0.0 copy-done.5
  15.3 0.0 copy-done.10
  15.3 0.0 copy-done.11
  15.3 0.0 copy-done.12
  15.3 0.0 copy-start.2
  15.3 0.9 %copy-done.2 = f32[4,16,640]{2,1,0:T(8,128)S(1)} copy-done((f32[4,16,640]{2,1,0:T(8,128)S(1)}, f32[4,16,640]{2,1,0:T(8,128)}, u32[]{:S(2)}) %copy-start.2) | copy-done | bytes 163864
  16.2 0.0 copy-start.3
  16.2 1.0 %copy-done.3 = f32[59,2048]{1,0:T(8,128)S(1)} copy-done((f32[59,2048]{1,0:T(8,128)S(1)}, f32[59,2048]{1,0:T(8,128)}, u32[]{:S(2)}) %copy-start.3) | copy-done | bytes 483352
  17.3 0.0 copy-start.4
  17.3 1.0 %copy-done.4 = f32[59,2048]{1,0:T(8,128)S(1)} copy-done((f32[59,2048]{1,0:T(8,128)S(1)}, f32[59,2048]{1,0:T(8,128)}, u32[]{:S(2)}) %copy-start.4) | copy-done | bytes 483352
  18.3 0.0 copy-start.6
  18.3 0.9 %copy-done.6 = f32[59,1024]{1,0:T(8,128)S(1)} copy-done((f32[59,1024]{1,0:T(8,128)S(1)}, f32[59,1024]{1,0:T(8,128)}, u32[]{:S(2)}) %copy-start.6) | copy-done | bytes 241688
  19.2 0.0 copy-start.7
  19.2 3.7 %update.1 = (f32[59,2048]{1,0:T(8,128)}, f32[59,2048]{1,0:T(8,128)}, f32[59,2048]{1,0:T(8,128)}, f32[64,8,128]{2,1,0:T(8,128)S(1)}, f32[16,1024]{1,0:T(8,128)S(1)}, /*index=5*/s32[1,1024]{1,0:T(1,128)S(1)}) custom-call(f32[4,16,640]{2,1,0:T(8,128)S(1)} %copy-done.2, f32[59,2048]{1,0:T(8,128)S(1)} %copy-done.1, f32[59,2048]{1,0:T(8,128)S(1)} %copy-done.3, ...), custom_call_target="tpu_custom_call" | custom-call | tf_op jit(solution)/shard_map/update/pallas_call | solution.py:527
  23.0 0.0 copy-done.7
  23.0 40.0 %consensus.1 = (f32[59,1024]{1,0:T(8,128)S(1)}, f32[59,1024]{1,0:T(8,128)S(1)}) custom-call(f32[64,8,128]{2,1,0:T(8,128)S(1)} %get-tuple-element.16.send, f32[59,1024]{1,0:T(8,128)S(1)} %copy-done.7, f32[16,1024]{1,0:T(8,128)S(1)} %get-tuple-element.17.holds, s32[1,1024]{1,0:T(1,128)S(1)} %get-tuple-element.18.place), custom_call_target="tpu_custom_call" | custom-call | tf_op jit(solution)/shard_map/consensus/pallas_call | solution.py:554
  63.0 0.7 %copy.22 = f32[59,1024]{1,0:T(8,128)} copy(f32[59,1024]{1,0:T(8,128)S(1)} %get-tuple-element.29) | data formatting | bytes 483328
  63.7 0.7 %copy.23 = f32[59,1024]{1,0:T(8,128)} copy(f32[59,1024]{1,0:T(8,128)S(1)} %get-tuple-element.30) | data formatting | bytes 483328
Async XLA Ops:
  0.6 1.0 %copy-start.9 = (f32[3,4096]{1,0:T(4,128)S(1)}, f32[3,4096]{1,0:T(4,128)}, u32[]{:S(2)}) copy-start(f32[3,4096]{1,0:T(4,128)} %target.1) | copy-start | bytes 147460
  1.6 1.0 %copy-start = (f32[59,2048]{1,0:T(8,128)S(1)}, f32[59,2048]{1,0:T(8,128)}, u32[]{:S(2)}) copy-start(f32[59,2048]{1,0:T(8,128)} %params.3) | copy-start | bytes 1449988
  2.7 0.7 %copy-start.13 = (f32[1,24]{1,0:T(1,128)S(1)}, f32[1,24]{1,0:T(1,128)}, u32[]{:S(2)}) copy-start(f32[1,24]{1,0:T(1,128)} %cam.1) | copy-start | bytes 292
  3.3 11.9 %copy-start.1 = (f32[59,2048]{1,0:T(8,128)S(1)}, f32[59,2048]{1,0:T(8,128)}, u32[]{:S(2)}) copy-start(f32[59,2048]{1,0:T(8,128)} %params.3) | copy-start | bytes 1449988
  3.3 11.9 %copy-start.5 = (f32[59,1024]{1,0:T(8,128)S(1)}, f32[59,1024]{1,0:T(8,128)}, u32[]{:S(2)}) copy-start(f32[59,1024]{1,0:T(8,128)} %dual.1) | copy-start | bytes 724996
  6.7 0.6 copy-start.8
  7.4 7.9 %copy-start.10 = (s32[1024]{0:T(1024)S(1)}, s32[1024]{0:T(1024)}, u32[]{:S(2)}) copy-start(s32[1024]{0:T(1024)} %param.19) | copy-start | bytes 12292
  7.4 7.9 %copy-start.11 = (s32[1024,1]{0,1:T(1,128)S(1)}, s32[1024,1]{0,1:T(1,128)}, u32[]{:S(2)}) copy-start(s32[1024,1]{0,1:T(1,128)} %param.20) | copy-start | bytes 12292
  7.4 7.9 %copy-start.12 = (s32[1024]{0:T(1024)S(1)}, s32[1024]{0:T(1024)}, u32[]{:S(2)}) copy-start(s32[1024]{0:T(1024)} %param.21) | copy-start | bytes 12292
  15.3 0.9 %copy-start.2 = (f32[4,16,640]{2,1,0:T(8,128)S(1)}, f32[4,16,640]{2,1,0:T(8,128)}, u32[]{:S(2)}) copy-start(f32[4,16,640]{2,1,0:T(8,128)} %exchange_views.1.gathered) | copy-start | bytes 491524
  16.2 1.0 %copy-start.3 = (f32[59,2048]{1,0:T(8,128)S(1)}, f32[59,2048]{1,0:T(8,128)}, u32[]{:S(2)}) copy-start(f32[59,2048]{1,0:T(8,128)} %moment1.1) | copy-start | bytes 1449988
  17.3 1.0 %copy-start.4 = (f32[59,2048]{1,0:T(8,128)S(1)}, f32[59,2048]{1,0:T(8,128)}, u32[]{:S(2)}) copy-start(f32[59,2048]{1,0:T(8,128)} %moment2.1) | copy-start | bytes 1449988
  18.3 0.9 %copy-start.6 = (f32[59,1024]{1,0:T(8,128)S(1)}, f32[59,1024]{1,0:T(8,128)}, u32[]{:S(2)}) copy-start(f32[59,1024]{1,0:T(8,128)} %z_copy.1) | copy-start | bytes 724996
  19.2 3.7 %copy-start.7 = (f32[59,1024]{1,0:T(8,128)S(1)}, f32[59,1024]{1,0:T(8,128)}, u32[]{:S(2)}) copy-start(f32[59,1024]{1,0:T(8,128)} %z_table.1) | copy-start | bytes 724996
where the time goes:
time: 64.8 us; the launch traced here: 64.4 us
  Pallas kernels  55 us (85%)
  local copies, waits for them, and re-layouts  7.87 us (12%)
  other arithmetic  0.8 us (1%)
  between operations  0.74 us (1%)
    pallas_call x1, Pallas kernels, local(): pl.pallas_call(consensus_kernel, out_shape=(shape((NPAR, ROWS), F32), sha...  40 us
    pallas_call x1, Pallas kernels, local(): pl.pallas_call(views_kernel, out_shape=shape((NVIEW, 16, WIDE), F32), in_...  7.85 us
    unnamed x30, local copies, waits for them, and re-layouts  7.71 us
    pallas_call x1, Pallas kernels, local(): pl.pallas_call(update_kernel, out_shape=(shape((NPAR, GAUSS), F32), shape...  3.74 us
    pallas_call x1, Pallas kernels, local(): pl.pallas_call(render_kernel, out_shape=shape((16, WIDE), F32), in_specs=...  3.42 us

commit v1 on v0

v1 whole, which is shorter than its diff:
```python
import functools

import jax
import jax.numpy as jnp
from jax import lax
from jax.experimental import pallas as pl
from jax.experimental.pallas import tpu as pltpu
from jax.sharding import PartitionSpec as P

LEARN = 0.05
BETA_ONE = 0.9
BETA_TWO = 0.999
EPSILON = 1e-08

NPAR = 59
GAUSS = 2048
COPIES = 1024
ROWS = 1024
TILES = 16
DEPTH = 32
PAIRS = TILES * DEPTH
PIXELS = 256
NBLK = 64
NVIEW = 4
CAP = 64
SHARE = 15
WIDE = PAIRS + 128
JOINT = NVIEW * PAIRS + COPIES
UNROLL = 4

F32 = jnp.float32
BF16 = jnp.bfloat16
I32 = jnp.int32
MESH = pl.DeviceIdType.MESH
NT = (((1,), (1,)), ((), ()))


def lane_gather(source, index, groups):
    low = index & 127
    high = index >> 7
    found = [jnp.take_along_axis(part, low, axis=1) for part in source[0]]
    for g in range(1, groups):
        here = high == g
        for n, part in enumerate(source[g]):
            found[n] = jnp.where(here, jnp.take_along_axis(part, low, axis=1), found[n])
    return found


def wide(row):
    return jnp.broadcast_to(row, (8, row.shape[1]))


def split(value):
    high = value.astype(BF16)
    return high, (value - high.astype(F32)).astype(BF16)


def share_of(ref, view):
    parts = [ref[SHARE * v : SHARE * v + 16, :] for v in range(NVIEW - 1)]
    rest = ref[SHARE * 3 : NPAR, :]
    result = jnp.concatenate([rest, jnp.zeros((16 - rest.shape[0], rest.shape[1]), rest.dtype)], axis=0)
    for v in range(3):
        result = jnp.where(view == v, parts[v], result)
    return result


def render(cam, params, lists, counts, target, table, sheet, goal, e_all, t_all, parts):
    table[0:11, :] = params[0:11, :]
    table[14:16, :] = jnp.zeros((2, GAUSS), F32)
    for c in range(3):
        colour = cam[0, 8] * params[11 + 16 * c : 12 + 16 * c, :]
        for k in range(1, 16):
            row = 11 + 16 * c + k
            colour += cam[0, 8 + k] * params[row : row + 1, :]
        table[11 + c : 12 + c, :] = colour + 0.5
    for c in range(3):
        for t in range(TILES):
            goal[16 * c + t : 16 * c + t + 1, :] = target[c : c + 1, PIXELS * t : PIXELS * (t + 1)]

    turned = lists[...].astype(F32).T
    slots = lax.broadcasted_iota(I32, (DEPTH, TILES), 0)
    turned = jnp.where(slots < counts[...], turned, turned + GAUSS)
    turned = jnp.concatenate([turned, jnp.zeros((DEPTH, 128 - TILES), F32)], axis=1)
    turns = [turned] + [pltpu.roll(turned, TILES * m, 1) for m in range(1, 8)]
    lane = lax.broadcasted_iota(I32, (1, 128), 1)
    pieces = []
    for j in range(PAIRS // 128):
        row = turns[0][8 * j : 8 * j + 1, :]
        for m in range(1, 8):
            row = jnp.where(lane >> 4 == m, turns[m][8 * j + m : 8 * j + m + 1, :], row)
        pieces.append(row)
    coded = jnp.concatenate(pieces, axis=1).astype(I32)
    live = jnp.where(coded < GAUSS, 1.0, 0.0)
    index = coded & (GAUSS - 1)
    picked = []
    for j in range(PAIRS // 128):
        lanes = wide(index[:, 128 * j : 128 * (j + 1)])
        source = [
            [table[8 * n : 8 * n + 8, 128 * g : 128 * (g + 1)] for n in range(2)]
            for g in range(GAUSS // 128)
        ]
        picked.append(jnp.concatenate(lane_gather(source, lanes, GAUSS // 128), axis=0))
    picked = jnp.concatenate(picked, axis=1)

    def take(row):
        return picked[row : row + 1, :]

    jac = [[cam[0, 3 * i + j] for j in range(3)] for i in range(2)]
    centre = [take(j) for j in range(3)]
    scale = [jnp.exp(take(3 + k)) for k in range(3)]
    quat = [take(6 + k) for k in range(4)]
    norm = 1.0 / jnp.sqrt(quat[0] * quat[0] + quat[1] * quat[1] + quat[2] * quat[2] + quat[3] * quat[3])
    qw, qx, qy, qz = [q * norm for q in quat]
    rot = [
        [1 - 2 * (qy * qy + qz * qz), 2 * (qx * qy - qw * qz), 2 * (qx * qz + qw * qy)],
        [2 * (qx * qy + qw * qz), 1 - 2 * (qx * qx + qz * qz), 2 * (qy * qz - qw * qx)],
        [2 * (qx * qz - qw * qy), 2 * (qy * qz + qw * qx), 1 - 2 * (qx * qx + qy * qy)],
    ]
    mixed = [
        [(jac[i][0] * rot[0][k] + jac[i][1] * rot[1][k] + jac[i][2] * rot[2][k]) * scale[k] for k in range(3)]
        for i in range(2)
    ]

    def inner(a, b):
        return a[0] * b[0] + a[1] * b[1] + a[2] * b[2]

    first = inner(mixed[0], mixed[0]) + 0.01
    second = inner(mixed[1], mixed[1]) + 0.01
    cross = inner(mixed[0], mixed[1])
    det = first * second - cross * cross
    con0, con1, con2 = second / det, -cross / det, first / det
    cu = inner(jac[0], centre) + cam[0, 6]
    cw = inner(jac[1], centre) + cam[0, 7]
    opacity = 1.0 / (1.0 + jnp.exp(-take(10)))
    shown = opacity * live

    rows = [cu, cw, con0, 2.0 * con1, con2, shown, take(11), take(12), take(13)]
    rows = jnp.concatenate(rows + [jnp.zeros((7, PAIRS), F32)], axis=0)
    sheet[...] = rows.T

    tile = lax.broadcasted_iota(I32, (TILES, PIXELS), 0)
    pixel = lax.broadcasted_iota(I32, (TILES, PIXELS), 1)
    pos_u = (((tile & 3) * 16 + (pixel & 15)).astype(F32) + 0.5) / 32.0 - 1.0
    pos_w = (((tile >> 2) * 16 + (pixel >> 4)).astype(F32) + 0.5) / 32.0 - 1.0

    def at_slot(s):
        return pl.ds(pl.multiple_of(TILES * s, TILES), TILES)

    def column(s, f):
        return jnp.broadcast_to(sheet[at_slot(s), f : f + 1], (TILES, PIXELS))

    def forward(step, state):
        image, passed = list(state[0:3]), state[3]
        for s in [UNROLL * step + n for n in range(UNROLL)]:
            du = pos_u - column(s, 0)
            dw = pos_w - column(s, 1)
            quad = (column(s, 2) * du + column(s, 3) * dw) * du + column(s, 4) * dw * dw
            bell = jnp.exp(-0.5 * quad)
            alpha = jnp.minimum(column(s, 5) * bell, 0.99)
            weight = alpha * passed
            for c in range(3):
                image[c] = image[c] + column(s, 6 + c) * weight
            e_all[at_slot(s), :] = bell
            t_all[at_slot(s), :] = passed
            passed = passed - weight
        return (*image, passed)

    zero = jnp.zeros((TILES, PIXELS), F32)
    image = lax.fori_loop(0, DEPTH // UNROLL, forward, (zero, zero, zero, zero + 1.0))
    diff = [image[c] - goal[16 * c : 16 * c + 16, :] for c in range(3)]

    def backward(step, behind):
        for s in [DEPTH - 1 - UNROLL * step - n for n in range(UNROLL)]:
            bell = e_all[at_slot(s), :]
            before = t_all[at_slot(s), :]
            raw = column(s, 5) * bell
            alpha = jnp.minimum(raw, 0.99)
            glow = diff[0] * column(s, 6) + diff[1] * column(s, 7) + diff[2] * column(s, 8)
            slope = before * (glow - behind)
            slope = jnp.where(raw < 0.99, slope, jnp.where(raw == 0.99, 0.5 * slope, 0.0))
            behind = behind + alpha * (glow - behind)
            weight = alpha * before
            sums = [-0.5 * raw * slope, bell * slope] + [diff[c] * weight for c in range(3)]
            for n, value in enumerate(sums):
                high, low = split(value)
                parts[2 * n, at_slot(s), :] = high
                parts[2 * n + 1, at_slot(s), :] = low
        return behind

    lax.fori_loop(0, DEPTH // UNROLL, backward, zero)

    which = lax.broadcasted_iota(I32, (16, PIXELS), 0)
    place = lax.broadcasted_iota(I32, (16, PIXELS), 1)
    in_u = ((place & 15).astype(F32) - 7.5) / 32.0
    in_w = ((place >> 4).astype(F32) - 7.5) / 32.0
    basis = jnp.where(which == 0, 1.0, 0.0)
    basis = jnp.where(which == 1, in_u, basis)
    basis = jnp.where(which == 2, in_w, basis)
    basis = jnp.where(which == 3, in_u * in_u, basis)
    basis = jnp.where(which == 4, in_u * in_w, basis)
    basis = jnp.where(which == 5, in_w * in_w, basis)
    basis = basis.astype(BF16)

    def over_pixels(n):
        return lax.dot_general(basis, parts[2 * n], NT, preferred_element_type=F32) + lax.dot_general(
            basis, parts[2 * n + 1], NT, preferred_element_type=F32
        )

    moments = over_pixels(0)
    m1, mu, mw, muu, muw, mww = [moments[n : n + 1, :] for n in range(6)]
    g_opacity = over_pixels(1)[0:1, :] * live
    g_colour = [over_pixels(2 + c)[0:1, :] for c in range(3)]
    at = lax.broadcasted_iota(I32, (1, PAIRS), 1) & 15
    off_u = cu - (((at & 3) * 16 + 8).astype(F32) / 32.0 - 1.0)
    off_w = cw - (((at >> 2) * 16 + 8).astype(F32) / 32.0 - 1.0)
    s_u = mu - off_u * m1
    s_w = mw - off_w * m1
    g_con0 = muu - off_u * (mu + s_u)
    g_con1 = 2.0 * (muw - off_u * mw - off_w * s_u)
    g_con2 = mww - off_w * (mw + s_w)
    g_cu = -2.0 * (con0 * s_u + con1 * s_w)
    g_cw = -2.0 * (con1 * s_u + con2 * s_w)

    g_first = -(con0 * con0 * g_con0 + con0 * con1 * g_con1 + con1 * con1 * g_con2)
    g_second = -(con1 * con1 * g_con0 + con1 * con2 * g_con1 + con2 * con2 * g_con2)
    g_cross = -(2.0 * con0 * con1 * g_con0 + (con0 * con2 + con1 * con1) * g_con1 + 2.0 * con1 * con2 * g_con2)
    g_mixed = [
        [2.0 * g_first * mixed[0][k] + g_cross * mixed[1][k] for k in range(3)],
        [2.0 * g_second * mixed[1][k] + g_cross * mixed[0][k] for k in range(3)],
    ]
    g_scale = [g_mixed[0][k] * mixed[0][k] + g_mixed[1][k] * mixed[1][k] for k in range(3)]
    r = [
        [(jac[0][j] * g_mixed[0][k] + jac[1][j] * g_mixed[1][k]) * scale[k] for k in range(3)] for j in range(3)
    ]
    h_w = 2 * (qz * (r[1][0] - r[0][1]) + qy * (r[0][2] - r[2][0]) + qx * (r[2][1] - r[1][2]))
    h_x = 2 * (
        qy * (r[0][1] + r[1][0]) + qz * (r[0][2] + r[2][0]) + qw * (r[2][1] - r[1][2]) - 2 * qx * (r[1][1] + r[2][2])
    )
    h_y = 2 * (
        qx * (r[0][1] + r[1][0]) + qz * (r[1][2] + r[2][1]) + qw * (r[0][2] - r[2][0]) - 2 * qy * (r[0][0] + r[2][2])
    )
    h_z = 2 * (
        qx * (r[0][2] + r[2][0]) + qy * (r[1][2] + r[2][1]) + qw * (r[1][0] - r[0][1]) - 2 * qz * (r[0][0] + r[1][1])
    )
    along = qw * h_w + qx * h_x + qy * h_y + qz * h_z
    g_quat = [(h - q * along) * norm for h, q in ((h_w, qw), (h_x, qx), (h_y, qy), (h_z, qz))]
    g_centre = [jac[0][j] * g_cu + jac[1][j] * g_cw for j in range(3)]
    g_logit = g_opacity * opacity * (1.0 - opacity)
    sent = g_centre + g_scale + g_quat + [g_logit] + g_colour + [index.astype(F32), jnp.zeros((1, PAIRS), F32)]
    spot = lax.broadcasted_iota(I32, (16, 128), 0)
    colbasis = jnp.zeros((16, 128), F32)
    for k in range(16):
        colbasis = jnp.where(spot == k, cam[0, 8 + k], colbasis)
    return jnp.concatenate(sent, axis=0), colbasis


def to_blocks(outgoing, incoming, send_sem, recv_sem, block):
    def one(k, _):
        other = (block + k) % NBLK
        pltpu.make_async_remote_copy(
            src_ref=outgoing.at[other],
            dst_ref=incoming.at[block],
            send_sem=send_sem,
            recv_sem=recv_sem,
            device_id={"blocks": other},
            device_id_type=MESH,
        ).start()
        return 0

    lax.fori_loop(1, NBLK, one, 0)
    incoming[block] = outgoing[block]


def wait_blocks(outgoing, incoming, send_sem, recv_sem, block):
    whole = pltpu.make_async_remote_copy(
        src_ref=outgoing.at[pl.ds(0, NBLK - 1)],
        dst_ref=incoming.at[pl.ds(0, NBLK - 1)],
        send_sem=send_sem,
        recv_sem=recv_sem,
        device_id={"blocks": block},
        device_id_type=MESH,
    )
    whole.wait_send()
    whole.wait_recv()


def to_views(pieces, send_sem, recv_sem, view):
    copies = []
    for k in range(1, NVIEW):
        copy = pltpu.make_async_remote_copy(
            src_ref=pieces.at[view],
            dst_ref=pieces.at[view],
            send_sem=send_sem.at[k - 1],
            recv_sem=recv_sem.at[k - 1],
            device_id={"views": (view + k) % NVIEW},
            device_id_type=MESH,
        )
        copy.start()
        copies.append(copy)
    return copies


def unpack(chunks, j):
    lane = lax.broadcasted_iota(I32, (8, 128), 1)
    even, odd = chunks[2 * j], chunks[2 * j + 1]
    top = jnp.where(lane < CAP, even, pltpu.roll(odd, CAP, 1))
    bottom = jnp.where(lane < CAP, pltpu.roll(even, CAP, 1), odd)
    return top, bottom


def pack(top, bottom, chunks, j):
    lane = lax.broadcasted_iota(I32, (8, 128), 1)
    chunks[2 * j] = jnp.where(lane < CAP, top, pltpu.roll(bottom, CAP, 1))
    chunks[2 * j + 1] = jnp.where(lane < CAP, pltpu.roll(top, CAP, 1), bottom)


def row_blocks(value, groups):
    return [[value[8 * n : 8 * n + 8, 128 * g : 128 * (g + 1)] for n in range(2)] for g in range(groups)]


def adam(value, first, second, grad):
    first = BETA_ONE * first + (1.0 - BETA_ONE) * grad
    second = BETA_TWO * second + (1.0 - BETA_TWO) * grad * grad
    mhat = first * (1.0 / (1.0 - BETA_ONE**10))
    vhat = second * (1.0 / (1.0 - BETA_TWO**10))
    return value - LEARN * mhat / (jnp.sqrt(vhat) + EPSILON), first, second


def round_kernel(
    cam, params_in, moment1_in, moment2_in, dual_in, z_copy_in, z_table_in, rows_in, owner_in, slot_in,
    lists_in, counts_in, target_in,
    params_out, moment1_out, moment2_out, z_out, dual_out,
    params, moment1, moment2, dual, z_copy, z_table, rows, owner, slot, lists, counts, target,
    table, sheet, goal, e_all, t_all, parts, gathered,
    left, masks, masked, onehot, source, names, place,
    send, got, answers, returned, z_parts, d_parts, items, item_masked, item_hot, z_new, dual_new,
    in_sem, out_sem, s_mine, r_mine, s_send, r_send, s_back, r_back, s_z, r_z, s_d, r_d,
):
    block = lax.axis_index("blocks")
    view = lax.axis_index("views")

    pairs = [
        (lists_in, lists), (counts_in, counts), (params_in, params), (target_in, target),
        (rows_in, rows), (owner_in, owner), (slot_in, slot), (dual_in, dual), (z_copy_in, z_copy),
        (moment1_in, moment1), (moment2_in, moment2), (z_table_in, z_table),
    ]
    arriving = [pltpu.make_async_copy(there, here, in_sem.at[n]) for n, (there, here) in enumerate(pairs)]
    for copy in arriving:
        copy.start()
    barrier = pltpu.get_barrier_semaphore()

    def greet(k, _):
        pl.semaphore_signal(barrier, inc=1, device_id={"blocks": (block + k) % NBLK}, device_id_type=MESH)
        return 0

    lax.fori_loop(1, NBLK, greet, 0)
    for k in range(1, NVIEW):
        pl.semaphore_signal(barrier, inc=1, device_id={"views": (view + k) % NVIEW}, device_id_type=MESH)

    for copy in arriving[0:4]:
        copy.wait()
    slots_part, basis_part = render(
        cam, params, lists, counts, target, table, sheet, goal, e_all, t_all, parts
    )
    gathered[view, :, 0:PAIRS] = slots_part
    gathered[view, :, PAIRS:WIDE] = basis_part
    pl.semaphore_wait(barrier, NBLK - 1 + NVIEW - 1)
    view_copies = to_views(gathered, s_mine, r_mine, view)

    for copy in arriving[4:]:
        copy.wait()
    owned = lax.broadcasted_iota(I32, (NBLK, COPIES), 0) == owner[...]
    owned = jnp.where(owned, 1.0, 0.0)
    upper = lax.broadcasted_iota(I32, (128, 128), 0) < lax.broadcasted_iota(I32, (128, 128), 1)
    upper = jnp.where(upper, 1.0, 0.0).astype(BF16)
    ranks = []
    carry = jnp.zeros((NBLK, 1), F32)
    for j in range(COPIES // 128):
        part = owned[:, 128 * j : 128 * (j + 1)]
        ahead = jnp.dot(part.astype(BF16), upper, preferred_element_type=F32) + carry
        ranks.append(jnp.sum(part * ahead, axis=0, keepdims=True))
        carry = carry + jnp.sum(part, axis=1, keepdims=True)
    rank = jnp.concatenate(ranks, axis=1).astype(I32)
    place[...] = owner[...] * CAP + rank
    ident = lax.broadcasted_iota(I32, (1, COPIES), 1)
    ranked = (lax.broadcasted_iota(I32, (128, COPIES), 0) & (CAP - 1)) == rank
    coarse = jnp.where(ranked, (ident >> 5).astype(F32), 0.0).astype(BF16)
    fine = jnp.where(ranked, ((ident & 31) + 1).astype(F32), 0.0).astype(BF16)
    owned = owned.astype(BF16)
    names[...] = (
        32.0 * lax.dot_general(owned, coarse, NT, preferred_element_type=F32)
        + lax.dot_general(owned, fine, NT, preferred_element_type=F32)
    ).astype(I32)

    boundary = rows[...]
    lanes = slice(NVIEW * PAIRS, JOINT)
    left[NPAR:64, :] = jnp.zeros((64 - NPAR, JOINT), F32)
    left[0:NPAR, lanes] = dual[...] - z_copy[...]
    left[NPAR : NPAR + 1, lanes] = jnp.ones((1, COPIES), F32)

    def prepare(index, lanes):
        width = index.shape[1]
        group = jnp.broadcast_to(index >> 8, (16, width))
        for h in range(8):
            masks[16 * h : 16 * h + 16, lanes] = jnp.where(group == h, 1.0, 0.0).astype(BF16)
        hot = lax.broadcasted_iota(I32, (256, width), 0) == (index & 255)
        onehot[:, lanes] = jnp.where(hot, 1.0, 0.0).astype(BF16)

    prepare(boundary, lanes)

    for copy in view_copies:
        copy.wait()
    for v in range(NVIEW):
        lanes = slice(PAIRS * v, PAIRS * (v + 1))
        left[0:11, lanes] = gathered[v, 0:11, 0:PAIRS]
        colbasis = gathered[v, :, PAIRS : PAIRS + 1]
        for c in range(3):
            left[11 + 16 * c : 27 + 16 * c, lanes] = colbasis * gathered[v, 11 + c : 12 + c, 0:PAIRS]
        prepare(gathered[v, 14:15, 0:PAIRS].astype(I32), lanes)

    spot = lax.broadcasted_iota(I32, (16, JOINT), 0)
    high, low = split(jnp.where(spot == 15, left[NPAR : NPAR + 1, :], share_of(left, view)))
    for h in range(8):
        mask = masks[16 * h : 16 * h + 16, :]
        masked[32 * h : 32 * h + 16, :] = high * mask
        masked[32 * h + 16 : 32 * h + 32, :] = low * mask
    total = lax.dot_general(masked[0:256, :], onehot[...], NT, preferred_element_type=F32)
    value, first, second = share_of(params, view), share_of(moment1, view), share_of(moment2, view)
    moved = []
    for h in range(8):
        both = total[32 * h : 32 * h + 16, :] + total[32 * h + 16 : 32 * h + 32, :]
        lanes = slice(256 * h, 256 * (h + 1))
        grad = both + both[15:16, :] * value[:, lanes]
        moved.append(adam(value[:, lanes], first[:, lanes], second[:, lanes], grad)[0])
    moved = row_blocks(jnp.concatenate(moved, axis=1), GAUSS // 128)
    fetched = []
    for j in range(COPIES // 128):
        found = lane_gather(moved, wide(boundary[:, 128 * j : 128 * (j + 1)]), GAUSS // 128)
        fetched.append(jnp.concatenate(found, axis=0))
    spot = lax.broadcasted_iota(I32, (16, COPIES), 0)
    sums = jnp.concatenate(fetched, axis=1) + share_of(dual, view)
    source[...] = jnp.where(spot == 15, (slot[...] + 1).astype(F32), sums)
    lane = lax.broadcasted_iota(I32, (8, 128), 1)
    blocks_of = row_blocks(source, COPIES // 128)
    for j in range(NBLK // 2):
        name = jnp.where(lane < CAP, wide(names[2 * j : 2 * j + 1, :]), wide(names[2 * j + 1 : 2 * j + 2, :]))
        top, bottom = lane_gather(blocks_of, jnp.maximum(name - 1, 0), COPIES // 128)
        pack(jnp.where(name > 0, top, 0.0), jnp.where(name > 0, bottom, 0.0), send, j)
    to_blocks(send, got, s_send, r_send, block)

    high, low = split(left[...])
    for h in range(8):
        mask = masks[16 * h : 16 * h + 16, :]
        for n in range(4):
            masked[128 * h + 16 * n : 128 * h + 16 * n + 16, :] = high[16 * n : 16 * n + 16, :] * mask
            masked[128 * h + 64 + 16 * n : 128 * h + 80 + 16 * n, :] = low[16 * n : 16 * n + 16, :] * mask
    total = lax.dot_general(masked[...], onehot[...], NT, preferred_element_type=F32)
    for h in range(8):
        both = total[128 * h : 128 * h + 64, :] + total[128 * h + 64 : 128 * h + 128, :]
        lanes = slice(256 * h, 256 * (h + 1))
        value = params[:, lanes]
        grad = both[0:NPAR] + both[NPAR : NPAR + 1] * value
        params[:, lanes], moment1[:, lanes], moment2[:, lanes] = adam(
            value, moment1[:, lanes], moment2[:, lanes], grad
        )
    leaving = [
        pltpu.make_async_copy(here, there, out_sem.at[n])
        for n, (here, there) in enumerate(
            [(params, params_out), (moment1, moment1_out), (moment2, moment2_out), (z_new, z_out), (dual_new, dual_out)]
        )
    ]
    for copy in leaving[0:3]:
        copy.start()
    mine = share_of(z_table, view)
    wait_blocks(send, got, s_send, r_send, block)

    for j in range(NBLK // 2):
        top, bottom = unpack(got, j)
        items[0:8, 128 * j : 128 * (j + 1)] = top
        items[8:16, 128 * j : 128 * (j + 1)] = bottom
    label = items[15:16, :].astype(I32)
    index = jnp.maximum(label - 1, 0)
    last = lax.broadcasted_iota(I32, (16, NBLK * CAP), 0) == 15
    high, low = split(jnp.where(last, 1.0, items[...]))
    group = jnp.broadcast_to(jnp.where(label > 0, index >> 8, 4), (16, NBLK * CAP))
    for h in range(4):
        mask = jnp.where(group == h, 1.0, 0.0).astype(BF16)
        item_masked[32 * h : 32 * h + 16, :] = high * mask
        item_masked[32 * h + 16 : 32 * h + 32, :] = low * mask
    hot = lax.broadcasted_iota(I32, (256, NBLK * CAP), 0) == (index & 255)
    item_hot[...] = jnp.where(hot, 1.0, 0.0).astype(BF16)
    total = lax.dot_general(item_masked[...], item_hot[...], NT, preferred_element_type=F32)
    fresh = []
    for h in range(4):
        both = total[32 * h : 32 * h + 16, :] + total[32 * h + 16 : 32 * h + 32, :]
        fresh.append((mine[:, 256 * h : 256 * (h + 1)] + both) / (1.0 + both[15:16, :]))
    fresh = jnp.concatenate(fresh, axis=1)
    z_parts[view] = fresh
    answer = row_blocks(fresh, ROWS // 128)
    for j in range(NBLK // 2):
        top, bottom = lane_gather(answer, wide(index[:, 128 * j : 128 * (j + 1)]), ROWS // 128)
        pack(top, bottom, answers, j)
    to_blocks(answers, returned, s_back, r_back, block)
    z_copies = to_views(z_parts, s_z, r_z, view)
    for copy in z_copies:
        copy.wait()
    for v in range(NVIEW):
        count = min(SHARE, NPAR - SHARE * v)
        z_new[SHARE * v : SHARE * v + count, :] = z_parts[v, 0:count, :]
    leaving[3].start()
    wait_blocks(answers, returned, s_back, r_back, block)

    for j in range(NBLK // 2):
        top, bottom = unpack(returned, j)
        items[0:8, 128 * j : 128 * (j + 1)] = top
        items[8:16, 128 * j : 128 * (j + 1)] = bottom
    fetched = []
    answer = row_blocks(items, NBLK // 2)
    for j in range(COPIES // 128):
        found = lane_gather(answer, wide(place[:, 128 * j : 128 * (j + 1)]), NBLK // 2)
        fetched.append(jnp.concatenate(found, axis=0))
    d_parts[view] = source[...] - jnp.concatenate(fetched, axis=1)
    d_copies = to_views(d_parts, s_d, r_d, view)
    for copy in d_copies:
        copy.wait()
    for v in range(NVIEW):
        count = min(SHARE, NPAR - SHARE * v)
        dual_new[SHARE * v : SHARE * v + count, :] = d_parts[v, 0:count, :]
    leaving[4].start()
    for copy in leaving:
        copy.wait()


def finish_kernel(*refs):
    sources, targets, staged, in_sem, out_sem = refs[0:5], refs[5:10], refs[10:15], refs[15], refs[16]
    steps = []
    for n, ref in enumerate(sources):
        for piece in range(ref.shape[1] // ROWS):
            lanes = pl.ds(ROWS * piece, ROWS)
            at = len(steps)
            steps.append(
                (
                    pltpu.make_async_copy(ref.at[:, lanes], staged[n].at[:, lanes], in_sem.at[at]),
                    pltpu.make_async_copy(staged[n].at[:, lanes], targets[n].at[:, lanes], out_sem.at[at]),
                )
            )
    for arrive, _ in steps:
        arrive.start()
    for arrive, leave in steps:
        arrive.wait()
        leave.start()
    for _, leave in steps:
        leave.wait()


def anywhere():
    return pl.BlockSpec(memory_space=pl.ANY)


def local(
    params, moment1, moment2, dual, z_copy, z_table, boundary_rows, owner_block, owner_slot,
    tile_lists, tile_counts, cameras, target,
):
    shape = jax.ShapeDtypeStruct
    outs = (shape((NPAR, GAUSS), F32),) * 3 + (shape((NPAR, ROWS), F32), shape((NPAR, COPIES), F32))

    def f32(*dims):
        return pltpu.VMEM(dims, F32)

    def bf16(*dims):
        return pltpu.VMEM(dims, BF16)

    def i32(*dims):
        return pltpu.VMEM(dims, I32)

    chunks = f32(NBLK, 8, 128)
    dma = pltpu.SemaphoreType.DMA
    results = pl.pallas_call(
        round_kernel,
        out_shape=outs,
        in_specs=[pl.BlockSpec(memory_space=pltpu.SMEM)] + [anywhere()] * 12,
        out_specs=(anywhere(),) * 5,
        scratch_shapes=[
            f32(NPAR, GAUSS), f32(NPAR, GAUSS), f32(NPAR, GAUSS),
            f32(NPAR, COPIES), f32(NPAR, COPIES), f32(NPAR, ROWS),
            i32(1, COPIES), i32(1, COPIES), i32(1, COPIES), i32(TILES, DEPTH), i32(1, TILES), f32(3, TILES * PIXELS),
            f32(16, GAUSS), f32(PAIRS, 16), f32(48, PIXELS), f32(PAIRS, PIXELS), f32(PAIRS, PIXELS),
            bf16(10, PAIRS, PIXELS), f32(NVIEW, 16, WIDE),
            f32(64, JOINT), bf16(128, JOINT), bf16(1024, JOINT), bf16(256, JOINT),
            f32(16, COPIES), i32(NBLK, 128), i32(1, COPIES),
            chunks, chunks, chunks, chunks, f32(NVIEW, 16, ROWS), f32(NVIEW, 16, COPIES),
            f32(16, NBLK * CAP), bf16(128, NBLK * CAP), bf16(256, NBLK * CAP), f32(NPAR, ROWS), f32(NPAR, COPIES),
            dma((12,)), dma((5,)), dma((3,)), dma((3,)), dma, dma, dma, dma, dma((3,)), dma((3,)), dma((3,)), dma((3,)),
        ],
        compiler_params=pltpu.CompilerParams(
            collective_id=0, has_side_effects=True, vmem_limit_bytes=56 * 1024 * 1024
        ),
        name="round",
    )(
        cameras, params, moment1, moment2, dual, z_copy, z_table,
        boundary_rows.reshape(1, COPIES), owner_block.reshape(1, COPIES), owner_slot.reshape(1, COPIES),
        tile_lists, tile_counts.reshape(1, TILES), target,
    )
    return pl.pallas_call(
        finish_kernel,
        out_shape=outs,
        in_specs=[anywhere()] * 5,
        out_specs=(anywhere(),) * 5,
        scratch_shapes=[f32(*out.shape) for out in outs] + [dma((8,)), dma((8,))],
        compiler_params=pltpu.CompilerParams(vmem_limit_bytes=56 * 1024 * 1024),
        name="finish",
    )(*results)


def solution(mesh):
    whole, both = P(None, "blocks"), ("blocks", "views")
    placed = (whole,) * 6 + (P("blocks"), P("blocks", None), P("blocks"))
    placed += (P(both, None), P(both), P(both, None), P(None, both))
    return jax.shard_map(local, mesh=mesh, in_specs=placed, out_specs=(whole,) * 5, check_vma=False)
```

time: 64.8 us -> 51.4 us (0.79)
  local copies, waits for them, and re-layouts: 7.87 us -> 0 us
  Pallas kernels: 55 us -> 50.7 us
  other arithmetic: 0.8 us -> 0 us
    unnamed x30 -> x0, local copies, waits for them, and re-layouts: 7.71 us -> none
    pallas_call x4 -> x2, Pallas kernels: 55 us -> 50.7 us  [the longest x1 48.3 us: local(): pl.pallas_call(round_kernel, out_shape=outs, in_specs=[pl.BlockSpec(memor...]
    transpose x1 -> x0, other arithmetic: 0.8 us -> none  [local(): jnp.where(spots < tile_counts[:, None], tile_lists, tile_lists + GAUSS)]
where the time goes in v1:
time: 51.4 us; the launch traced here: 51.3 us
  Pallas kernels  50.7 us (99%)
  between operations  0.64 us (1%)
    pallas_call x1, Pallas kernels, local(): pl.pallas_call(round_kernel, out_shape=outs, in_specs=[pl.BlockSpec(memor...  48.3 us
    pallas_call x1, Pallas kernels, local(): pl.pallas_call(finish_kernel, out_shape=outs, in_specs=[anywhere()] * 5,...  2.4 us

profile of v1, /device:TPU:1, one launch (start us, length us, event | category | flops | bytes accessed | tf_op | source)
XLA Modules:
  0.0 51.3 jit_solution(2508742056288819247)
XLA Ops:
  0.6 48.3 %round.1 = (f32[59,2048]{1,0:T(8,128)}, f32[59,2048]{1,0:T(8,128)}, f32[59,2048]{1,0:T(8,128)}, f32[59,1024]{1,0:T(8,128)}, f32[59,1024]{1,0:T(8,128)}) custom-call(f32[1,24]{1,0:T(1,128)} %cam.1, f32[59,2048]{1,0:T(8,128)} %params_in.1, f32[59,2048]{1,0:T(8,128)} %moment1_in.1, f32[59,2048]{1,0:T(8,128)} %moment2_in.1, f32[59,1024]{1,0:T(8,128)} %dual_in.1, ...), custom_call_target="tpu_custom_call" | custom-call | tf_op jit(solution)/shard_map/round/pallas_call | solution.py:578
  48.9 2.4 %finish.1 = (f32[59,2048]{1,0:T(8,128)}, f32[59,2048]{1,0:T(8,128)}, f32[59,2048]{1,0:T(8,128)}, f32[59,1024]{1,0:T(8,128)}, f32[59,1024]{1,0:T(8,128)}) custom-call(f32[59,2048]{1,0:T(8,128)} %get-tuple-element.10.refs_0_, f32[59,2048]{1,0:T(8,128)} %get-tuple-element.11.refs_1_, f32[59,2048]{1,0:T(8,128)} %get-tuple-element.12.refs_2_, ...), custom_call_target="tpu_custom_call" | custom-call | tf_op jit(solution)/shard_map/finish/pallas_call | solution.py:604

commit v2 on v1

--- a/solution.py
+++ b/solution.py
@@ -24,7 +24,6 @@
 NVIEW = 4
 CAP = 64
 SHARE = 15
-WIDE = PAIRS + 128
 JOINT = NVIEW * PAIRS + COPIES
 UNROLL = 4
 
@@ -35,15 +34,23 @@
 NT = (((1,), (1,)), ((), ()))
 
 
-def lane_gather(source, index, groups):
+def lane_gather(source, index):
     low = index & 127
     high = index >> 7
-    found = [jnp.take_along_axis(part, low, axis=1) for part in source[0]]
-    for g in range(1, groups):
-        here = high == g
-        for n, part in enumerate(source[g]):
-            found[n] = jnp.where(here, jnp.take_along_axis(part, low, axis=1), found[n])
+    found = jnp.take_along_axis(source[0], low, axis=1)
+    for g in range(1, len(source)):
+        found = jnp.where(high == g, jnp.take_along_axis(source[g], low, axis=1), found)
     return found
+
+
+def groups_of(value, rows):
+    return [value[rows : rows + 8, 128 * g : 128 * (g + 1)] for g in range(value.shape[1] // 128)]
+
+
+def fetch(value, rows, index):
+    source = groups_of(value, rows)
+    found = [lane_gather(source, wide(index[:, 128 * j : 128 * (j + 1)])) for j in range(index.shape[1] // 128)]
+    return jnp.concatenate(found, axis=1)
 
 
 def wide(row):
@@ -56,12 +63,23 @@
 
 
 def share_of(ref, view):
-    parts = [ref[SHARE * v : SHARE * v + 16, :] for v in range(NVIEW - 1)]
-    rest = ref[SHARE * 3 : NPAR, :]
-    result = jnp.concatenate([rest, jnp.zeros((16 - rest.shape[0], rest.shape[1]), rest.dtype)], axis=0)
+    parts = []
+    for v in range(NVIEW):
+        end = min(SHARE * v + SHARE, NPAR)
+        rows = [ref[SHARE * v : SHARE * v + 7, :], jnp.zeros((1, ref.shape[1]), F32), ref[SHARE * v + 7 : end, :]]
+        if end < SHARE * v + SHARE:
+            rows.append(jnp.zeros((SHARE * v + SHARE - end, ref.shape[1]), F32))
+        parts.append(jnp.concatenate(rows, axis=0))
+    result = parts[3]
     for v in range(3):
         result = jnp.where(view == v, parts[v], result)
     return result
+
+
+def assemble(target, part, v, wave):
+    start = SHARE * v + 7 * wave
+    count = min(7 + wave, NPAR - start)
+    target[start : start + count, :] = part[0:count, :]
 
 
 def render(cam, params, lists, counts, target, table, sheet, goal, e_all, t_all, parts):
@@ -95,11 +113,7 @@
     picked = []
     for j in range(PAIRS // 128):
         lanes = wide(index[:, 128 * j : 128 * (j + 1)])
-        source = [
-            [table[8 * n : 8 * n + 8, 128 * g : 128 * (g + 1)] for n in range(2)]
-            for g in range(GAUSS // 128)
-        ]
-        picked.append(jnp.concatenate(lane_gather(source, lanes, GAUSS // 128), axis=0))
+        picked.append(jnp.concatenate([lane_gather(groups_of(table, 8 * n), lanes) for n in range(2)], axis=0))
     picked = jnp.concatenate(picked, axis=1)
 
     def take(row):
@@ -246,37 +260,37 @@
     g_quat = [(h - q * along) * norm for h, q in ((h_w, qw), (h_x, qx), (h_y, qy), (h_z, qz))]
     g_centre = [jac[0][j] * g_cu + jac[1][j] * g_cw for j in range(3)]
     g_logit = g_opacity * opacity * (1.0 - opacity)
-    sent = g_centre + g_scale + g_quat + [g_logit] + g_colour + [index.astype(F32), jnp.zeros((1, PAIRS), F32)]
-    spot = lax.broadcasted_iota(I32, (16, 128), 0)
-    colbasis = jnp.zeros((16, 128), F32)
+    along_row = lax.broadcasted_iota(I32, (1, PAIRS), 1)
+    colbasis = jnp.zeros((1, PAIRS), F32)
     for k in range(16):
-        colbasis = jnp.where(spot == k, cam[0, 8 + k], colbasis)
-    return jnp.concatenate(sent, axis=0), colbasis
-
-
-def to_blocks(outgoing, incoming, send_sem, recv_sem, block):
+        colbasis = jnp.where(along_row == k, cam[0, 8 + k], colbasis)
+    sent = g_centre + g_scale + g_quat + [g_logit] + g_colour + [index.astype(F32), colbasis]
+    return jnp.concatenate(sent, axis=0)
+
+
+def to_blocks(outgoing, incoming, send_sem, recv_sem, block, wave):
     def one(k, _):
         other = (block + k) % NBLK
         pltpu.make_async_remote_copy(
-            src_ref=outgoing.at[other],
-            dst_ref=incoming.at[block],
-            send_sem=send_sem,
-            recv_sem=recv_sem,
+            src_ref=outgoing.at[wave, other],
+            dst_ref=incoming.at[wave, block],
+            send_sem=send_sem.at[wave],
+            recv_sem=recv_sem.at[wave],
             device_id={"blocks": other},
             device_id_type=MESH,
         ).start()
         return 0
 
     lax.fori_loop(1, NBLK, one, 0)
-    incoming[block] = outgoing[block]
-
-
-def wait_blocks(outgoing, incoming, send_sem, recv_sem, block):
+    incoming[wave, block] = outgoing[wave, block]
+
+
+def wait_blocks(outgoing, incoming, send_sem, recv_sem, block, wave):
     whole = pltpu.make_async_remote_copy(
-        src_ref=outgoing.at[pl.ds(0, NBLK - 1)],
-        dst_ref=incoming.at[pl.ds(0, NBLK - 1)],
-        send_sem=send_sem,
-        recv_sem=recv_sem,
+        src_ref=outgoing.at[wave, pl.ds(0, NBLK - 1)],
+        dst_ref=incoming.at[wave, pl.ds(0, NBLK - 1)],
+        send_sem=send_sem.at[wave],
+        recv_sem=recv_sem.at[wave],
         device_id={"blocks": block},
         device_id_type=MESH,
     )
@@ -284,12 +298,12 @@
     whole.wait_recv()
 
 
-def to_views(pieces, send_sem, recv_sem, view):
+def to_views(piece, send_sem, recv_sem, view):
     copies = []
     for k in range(1, NVIEW):
         copy = pltpu.make_async_remote_copy(
-            src_ref=pieces.at[view],
-            dst_ref=pieces.at[view],
+            src_ref=piece,
+            dst_ref=piece,
             send_sem=send_sem.at[k - 1],
             recv_sem=recv_sem.at[k - 1],
             device_id={"views": (view + k) % NVIEW},
@@ -300,22 +314,20 @@
     return copies
 
 
-def unpack(chunks, j):
-    lane = lax.broadcasted_iota(I32, (8, 128), 1)
-    even, odd = chunks[2 * j], chunks[2 * j + 1]
-    top = jnp.where(lane < CAP, even, pltpu.roll(odd, CAP, 1))
-    bottom = jnp.where(lane < CAP, pltpu.roll(even, CAP, 1), odd)
-    return top, bottom
-
-
-def pack(top, bottom, chunks, j):
-    lane = lax.broadcasted_iota(I32, (8, 128), 1)
-    chunks[2 * j] = jnp.where(lane < CAP, top, pltpu.roll(bottom, CAP, 1))
-    chunks[2 * j + 1] = jnp.where(lane < CAP, pltpu.roll(top, CAP, 1), bottom)
-
-
-def row_blocks(value, groups):
-    return [[value[8 * n : 8 * n + 8, 128 * g : 128 * (g + 1)] for n in range(2)] for g in range(groups)]
+def refold(value):
+    left = lax.broadcasted_iota(I32, (8, 128), 1) < CAP
+    upper = lax.broadcasted_iota(I32, (8, 128), 0) < 4
+    return jnp.where(left == upper, value, pltpu.roll(pltpu.roll(value, CAP, 1), 4, 0))
+
+
+def pack(value, chunks, wave, j):
+    folded = refold(value)
+    chunks[wave, 2 * j] = folded[0:4]
+    chunks[wave, 2 * j + 1] = folded[4:8]
+
+
+def unpack(chunks, wave, j):
+    return refold(jnp.concatenate([chunks[wave, 2 * j], chunks[wave, 2 * j + 1]], axis=0))
 
 
 def adam(value, first, second, grad):
@@ -332,8 +344,8 @@
     params_out, moment1_out, moment2_out, z_out, dual_out,
     params, moment1, moment2, dual, z_copy, z_table, rows, owner, slot, lists, counts, target,
     table, sheet, goal, e_all, t_all, parts, gathered,
-    left, masks, masked, onehot, source, names, place,
-    send, got, answers, returned, z_parts, d_parts, items, item_masked, item_hot, z_new, dual_new,
+    left, masks, masked, pen_masked, onehot, source, names, place, s_value, s_first, s_second, s_dual, s_table,
+    send, got, answers, returned, z_parts, d_parts, items, item_masks, item_masked, item_hot, z_new, dual_new,
     in_sem, out_sem, s_mine, r_mine, s_send, r_send, s_back, r_back, s_z, r_z, s_d, r_d,
 ):
     block = lax.axis_index("blocks")
@@ -359,13 +371,9 @@
 
     for copy in arriving[0:4]:
         copy.wait()
-    slots_part, basis_part = render(
-        cam, params, lists, counts, target, table, sheet, goal, e_all, t_all, parts
-    )
-    gathered[view, :, 0:PAIRS] = slots_part
-    gathered[view, :, PAIRS:WIDE] = basis_part
+    gathered[view] = render(cam, params, lists, counts, target, table, sheet, goal, e_all, t_all, parts)
     pl.semaphore_wait(barrier, NBLK - 1 + NVIEW - 1)
-    view_copies = to_views(gathered, s_mine, r_mine, view)
+    view_copies = to_views(gathered.at[view], s_mine, r_mine, view)
 
     for copy in arriving[4:]:
         copy.wait()
@@ -408,45 +416,60 @@
 
     prepare(boundary, lanes)
 
+    s_value[...] = share_of(params, view)
+    s_first[...] = share_of(moment1, view)
+    s_second[...] = share_of(moment2, view)
+    s_dual[...] = share_of(dual, view)
+    s_table[...] = share_of(z_table, view)
+
+    def share_masked(target, value, at):
+        high, low = split(value)
+        for h in range(8):
+            mask = masks[16 * h : 16 * h + 16, at]
+            target[32 * h : 32 * h + 16, :] = high * mask
+            target[32 * h + 16 : 32 * h + 32, :] = low * mask
+
+    spot = lax.broadcasted_iota(I32, (16, COPIES), 0)
+    share_masked(pen_masked, jnp.where(spot == 7, 1.0, share_of(left.at[:, lanes], view)), lanes)
+    pen_total = lax.dot_general(pen_masked[...], onehot[:, lanes], NT, preferred_element_type=F32)
+
     for copy in view_copies:
         copy.wait()
+    diagonal = lax.broadcasted_iota(I32, (16, 128), 0) == lax.broadcasted_iota(I32, (16, 128), 1)
     for v in range(NVIEW):
         lanes = slice(PAIRS * v, PAIRS * (v + 1))
-        left[0:11, lanes] = gathered[v, 0:11, 0:PAIRS]
-        colbasis = gathered[v, :, PAIRS : PAIRS + 1]
+        left[0:11, lanes] = gathered[v, 0:11, :]
+        colbasis = jnp.sum(jnp.where(diagonal, gathered[v, 15:16, 0:128], 0.0), axis=1, keepdims=True)
         for c in range(3):
-            left[11 + 16 * c : 27 + 16 * c, lanes] = colbasis * gathered[v, 11 + c : 12 + c, 0:PAIRS]
-        prepare(gathered[v, 14:15, 0:PAIRS].astype(I32), lanes)
-
-    spot = lax.broadcasted_iota(I32, (16, JOINT), 0)
-    high, low = split(jnp.where(spot == 15, left[NPAR : NPAR + 1, :], share_of(left, view)))
-    for h in range(8):
-        mask = masks[16 * h : 16 * h + 16, :]
-        masked[32 * h : 32 * h + 16, :] = high * mask
-        masked[32 * h + 16 : 32 * h + 32, :] = low * mask
-    total = lax.dot_general(masked[0:256, :], onehot[...], NT, preferred_element_type=F32)
-    value, first, second = share_of(params, view), share_of(moment1, view), share_of(moment2, view)
+            left[11 + 16 * c : 27 + 16 * c, lanes] = colbasis * gathered[v, 11 + c : 12 + c, :]
+        prepare(gathered[v, 14:15, :].astype(I32), lanes)
+
+    lanes = slice(0, NVIEW * PAIRS)
+    view_masked = masked.at[0:256, lanes]
+    share_masked(view_masked, share_of(left.at[:, lanes], view), lanes)
+    total = pen_total + lax.dot_general(view_masked[...], onehot[:, lanes], NT, preferred_element_type=F32)
     moved = []
     for h in range(8):
         both = total[32 * h : 32 * h + 16, :] + total[32 * h + 16 : 32 * h + 32, :]
         lanes = slice(256 * h, 256 * (h + 1))
-        grad = both + both[15:16, :] * value[:, lanes]
-        moved.append(adam(value[:, lanes], first[:, lanes], second[:, lanes], grad)[0])
-    moved = row_blocks(jnp.concatenate(moved, axis=1), GAUSS // 128)
-    fetched = []
-    for j in range(COPIES // 128):
-        found = lane_gather(moved, wide(boundary[:, 128 * j : 128 * (j + 1)]), GAUSS // 128)
-        fetched.append(jnp.concatenate(found, axis=0))
-    spot = lax.broadcasted_iota(I32, (16, COPIES), 0)
-    sums = jnp.concatenate(fetched, axis=1) + share_of(dual, view)
-    source[...] = jnp.where(spot == 15, (slot[...] + 1).astype(F32), sums)
+        value = s_value[:, lanes]
+        grad = both + both[7:8, :] * value
+        moved.append(adam(value, s_first[:, lanes], s_second[:, lanes], grad)[0])
+    moved = jnp.concatenate(moved, axis=1)
     lane = lax.broadcasted_iota(I32, (8, 128), 1)
-    blocks_of = row_blocks(source, COPIES // 128)
-    for j in range(NBLK // 2):
-        name = jnp.where(lane < CAP, wide(names[2 * j : 2 * j + 1, :]), wide(names[2 * j + 1 : 2 * j + 2, :]))
-        top, bottom = lane_gather(blocks_of, jnp.maximum(name - 1, 0), COPIES // 128)
-        pack(jnp.where(name > 0, top, 0.0), jnp.where(name > 0, bottom, 0.0), send, j)
-    to_blocks(send, got, s_send, r_send, block)
+    spot = lax.broadcasted_iota(I32, (8, COPIES), 0)
+    for wave in range(2):
+        at = slice(8 * wave, 8 * wave + 8)
+        sums = fetch(moved, 8 * wave, boundary) + s_dual[at, :]
+        if wave == 0:
+            sums = jnp.where(spot == 7, (slot[...] + 1).astype(F32), sums)
+        source[at, :] = sums
+        blocks_of = groups_of(source, 8 * wave)
+        for j in range(NBLK // 2):
+            name = jnp.where(lane < CAP, wide(names[2 * j : 2 * j + 1, :]), wide(names[2 * j + 1 : 2 * j + 2, :]))
+            found = lane_gather(blocks_of, jnp.maximum(name - 1, 0))
+            pack(jnp.where(name > 0, found, 0.0), send, wave, j)
+        to_blocks(send, got, s_send, r_send, block, wave)
 
     high, low = split(left[...])
     for h in range(8):
@@ -471,61 +494,58 @@
     ]
     for copy in leaving[0:3]:
         copy.start()
-    mine = share_of(z_table, view)
-    wait_blocks(send, got, s_send, r_send, block)
-
-    for j in range(NBLK // 2):
-        top, bottom = unpack(got, j)
-        items[0:8, 128 * j : 128 * (j + 1)] = top
-        items[8:16, 128 * j : 128 * (j + 1)] = bottom
-    label = items[15:16, :].astype(I32)
-    index = jnp.maximum(label - 1, 0)
-    last = lax.broadcasted_iota(I32, (16, NBLK * CAP), 0) == 15
-    high, low = split(jnp.where(last, 1.0, items[...]))
-    group = jnp.broadcast_to(jnp.where(label > 0, index >> 8, 4), (16, NBLK * CAP))
-    for h in range(4):
-        mask = jnp.where(group == h, 1.0, 0.0).astype(BF16)
-        item_masked[32 * h : 32 * h + 16, :] = high * mask
-        item_masked[32 * h + 16 : 32 * h + 32, :] = low * mask
-    hot = lax.broadcasted_iota(I32, (256, NBLK * CAP), 0) == (index & 255)
-    item_hot[...] = jnp.where(hot, 1.0, 0.0).astype(BF16)
-    total = lax.dot_general(item_masked[...], item_hot[...], NT, preferred_element_type=F32)
-    fresh = []
-    for h in range(4):
-        both = total[32 * h : 32 * h + 16, :] + total[32 * h + 16 : 32 * h + 32, :]
-        fresh.append((mine[:, 256 * h : 256 * (h + 1)] + both) / (1.0 + both[15:16, :]))
-    fresh = jnp.concatenate(fresh, axis=1)
-    z_parts[view] = fresh
-    answer = row_blocks(fresh, ROWS // 128)
-    for j in range(NBLK // 2):
-        top, bottom = lane_gather(answer, wide(index[:, 128 * j : 128 * (j + 1)]), ROWS // 128)
-        pack(top, bottom, answers, j)
-    to_blocks(answers, returned, s_back, r_back, block)
-    z_copies = to_views(z_parts, s_z, r_z, view)
-    for copy in z_copies:
-        copy.wait()
-    for v in range(NVIEW):
-        count = min(SHARE, NPAR - SHARE * v)
-        z_new[SHARE * v : SHARE * v + count, :] = z_parts[v, 0:count, :]
-    leaving[3].start()
-    wait_blocks(answers, returned, s_back, r_back, block)
-
-    for j in range(NBLK // 2):
-        top, bottom = unpack(returned, j)
-        items[0:8, 128 * j : 128 * (j + 1)] = top
-        items[8:16, 128 * j : 128 * (j + 1)] = bottom
-    fetched = []
-    answer = row_blocks(items, NBLK // 2)
-    for j in range(COPIES // 128):
-        found = lane_gather(answer, wide(place[:, 128 * j : 128 * (j + 1)]), NBLK // 2)
-        fetched.append(jnp.concatenate(found, axis=0))
-    d_parts[view] = source[...] - jnp.concatenate(fetched, axis=1)
-    d_copies = to_views(d_parts, s_d, r_d, view)
-    for copy in d_copies:
-        copy.wait()
-    for v in range(NVIEW):
-        count = min(SHARE, NPAR - SHARE * v)
-        dual_new[SHARE * v : SHARE * v + count, :] = d_parts[v, 0:count, :]
+    last = lax.broadcasted_iota(I32, (8, NBLK * CAP), 0) == 7
+    for wave in range(2):
+        at = slice(8 * wave, 8 * wave + 8)
+        wait_blocks(send, got, s_send, r_send, block, wave)
+        for j in range(NBLK // 2):
+            items[at, 128 * j : 128 * (j + 1)] = unpack(got, wave, j)
+        value = items[at, :]
+        if wave == 0:
+            label = items[7:8, :].astype(I32)
+            index = jnp.maximum(label - 1, 0)
+            group = jnp.broadcast_to(jnp.where(label > 0, index >> 8, 4), (16, NBLK * CAP))
+            for h in range(4):
+                item_masks[16 * h : 16 * h + 16, :] = jnp.where(group == h, 1.0, 0.0).astype(BF16)
+            hot = lax.broadcasted_iota(I32, (256, NBLK * CAP), 0) == (index & 255)
+            item_hot[...] = jnp.where(hot, 1.0, 0.0).astype(BF16)
+            value = jnp.where(last, 1.0, value)
+        high = value.astype(BF16).astype(F32)
+        both = jnp.concatenate([high, value - high], axis=0).astype(BF16)
+        for h in range(4):
+            item_masked[16 * h : 16 * h + 16, :] = both * item_masks[16 * h : 16 * h + 16, :]
+        total = lax.dot_general(item_masked[...], item_hot[...], NT, preferred_element_type=F32)
+        total = jnp.concatenate([total[16 * h : 16 * h + 8, :] + total[16 * h + 8 : 16 * h + 16, :] for h in range(4)], axis=1)
+        if wave == 0:
+            number = 1.0 + total[7:8, :]
+        fresh = (s_table[at, :] + total) / number
+        z_parts[view, at, :] = fresh
+        answer = groups_of(fresh, 0)
+        for j in range(NBLK // 2):
+            pack(lane_gather(answer, wide(index[:, 128 * j : 128 * (j + 1)])), answers, wave, j)
+        to_blocks(answers, returned, s_back, r_back, block, wave)
+    z_copies = to_views(z_parts.at[view], s_z, r_z, view)
+
+    d_copies = []
+    for wave in range(2):
+        at = slice(8 * wave, 8 * wave + 8)
+        wait_blocks(answers, returned, s_back, r_back, block, wave)
+        for j in range(NBLK // 2):
+            items[at, 128 * j : 128 * (j + 1)] = unpack(returned, wave, j)
+        d_parts[wave, view] = source[at, :] - fetch(items, 8 * wave, place)
+        d_copies.append(to_views(d_parts.at[wave, view], s_d.at[wave], r_d.at[wave], view))
+        if wave == 0:
+            for copy in z_copies:
+                copy.wait()
+            for v in range(NVIEW):
+                for part in range(2):
+                    assemble(z_new, z_parts.at[v, 8 * part : 8 * part + 8], v, part)
+            leaving[3].start()
+    for wave in range(2):
+        for copy in d_copies[wave]:
+            copy.wait()
+        for v in range(NVIEW):
+            assemble(dual_new, d_parts.at[wave, v], v, wave)
     leaving[4].start()
     for copy in leaving:
         copy.wait()
@@ -573,7 +593,7 @@
     def i32(*dims):
         return pltpu.VMEM(dims, I32)
 
-    chunks = f32(NBLK, 8, 128)
+    chunks = f32(2, NBLK, 4, 128)
     dma = pltpu.SemaphoreType.DMA
     results = pl.pallas_call(
         round_kernel,
@@ -585,12 +605,14 @@
             f32(NPAR, COPIES), f32(NPAR, COPIES), f32(NPAR, ROWS),
             i32(1, COPIES), i32(1, COPIES), i32(1, COPIES), i32(TILES, DEPTH), i32(1, TILES), f32(3, TILES * PIXELS),
             f32(16, GAUSS), f32(PAIRS, 16), f32(48, PIXELS), f32(PAIRS, PIXELS), f32(PAIRS, PIXELS),
-            bf16(10, PAIRS, PIXELS), f32(NVIEW, 16, WIDE),
-            f32(64, JOINT), bf16(128, JOINT), bf16(1024, JOINT), bf16(256, JOINT),
+            bf16(10, PAIRS, PIXELS), f32(NVIEW, 16, PAIRS),
+            f32(64, JOINT), bf16(128, JOINT), bf16(1024, JOINT), bf16(256, COPIES), bf16(256, JOINT),
             f32(16, COPIES), i32(NBLK, 128), i32(1, COPIES),
-            chunks, chunks, chunks, chunks, f32(NVIEW, 16, ROWS), f32(NVIEW, 16, COPIES),
-            f32(16, NBLK * CAP), bf16(128, NBLK * CAP), bf16(256, NBLK * CAP), f32(NPAR, ROWS), f32(NPAR, COPIES),
-            dma((12,)), dma((5,)), dma((3,)), dma((3,)), dma, dma, dma, dma, dma((3,)), dma((3,)), dma((3,)), dma((3,)),
+            f32(16, GAUSS), f32(16, GAUSS), f32(16, GAUSS), f32(16, COPIES), f32(16, ROWS),
+            chunks, chunks, chunks, chunks, f32(NVIEW, 16, ROWS), f32(2, NVIEW, 8, COPIES),
+            f32(16, NBLK * CAP), bf16(64, NBLK * CAP), bf16(64, NBLK * CAP), bf16(256, NBLK * CAP), f32(NPAR, ROWS), f32(NPAR, COPIES),
+            dma((12,)), dma((5,)), dma((3,)), dma((3,)), dma((2,)), dma((2,)), dma((2,)), dma((2,)),
+            dma((3,)), dma((3,)), dma((2, 3)), dma((2, 3)),
         ],
         compiler_params=pltpu.CompilerParams(
             collective_id=0, has_side_effects=True, vmem_limit_bytes=56 * 1024 * 1024

time: 51.4 us -> 48.1 us (0.936)
  Pallas kernels: 50.7 us -> 47.3 us
    pallas_call x1, Pallas kernels: 48.3 us -> 44.9 us  [local(): pl.pallas_call(round_kernel, out_shape=outs, in_specs=[pl.BlockSpec(memor...]
where the time goes in v2:
time: 48.1 us; the launch traced here: 48 us
  Pallas kernels  47.3 us (98%)
  between operations  0.64 us (1%)
    pallas_call x1, Pallas kernels, local(): pl.pallas_call(round_kernel, out_shape=outs, in_specs=[pl.BlockSpec(memor...  44.9 us
    pallas_call x1, Pallas kernels, local(): pl.pallas_call(finish_kernel, out_shape=outs, in_specs=[anywhere()] * 5,...  2.4 us

profile of v2, /device:TPU:1, one launch (start us, length us, event | category | flops | bytes accessed | tf_op | source)
XLA Modules:
  0.0 48.0 jit_solution(10383843118062802279)
XLA Ops:
  0.6 44.9 %round.1 = (f32[59,2048]{1,0:T(8,128)}, f32[59,2048]{1,0:T(8,128)}, f32[59,2048]{1,0:T(8,128)}, f32[59,1024]{1,0:T(8,128)}, f32[59,1024]{1,0:T(8,128)}) custom-call(f32[1,24]{1,0:T(1,128)} %cam.1, f32[59,2048]{1,0:T(8,128)} %params_in.1, f32[59,2048]{1,0:T(8,128)} %moment1_in.1, f32[59,2048]{1,0:T(8,128)} %moment2_in.1, f32[59,1024]{1,0:T(8,128)} %dual_in.1, ...), custom_call_target="tpu_custom_call" | custom-call | tf_op jit(solution)/shard_map/round/pallas_call | solution.py:598
  45.6 2.4 %finish.1 = (f32[59,2048]{1,0:T(8,128)}, f32[59,2048]{1,0:T(8,128)}, f32[59,2048]{1,0:T(8,128)}, f32[59,1024]{1,0:T(8,128)}, f32[59,1024]{1,0:T(8,128)}) custom-call(f32[59,2048]{1,0:T(8,128)} %get-tuple-element.10.refs_0_, f32[59,2048]{1,0:T(8,128)} %get-tuple-element.11.refs_1_, f32[59,2048]{1,0:T(8,128)} %get-tuple-element.12.refs_2_, ...), custom_call_target="tpu_custom_call" | custom-call | tf_op jit(solution)/shard_map/finish/pallas_call | solution.py:626

commit v3 on v2

--- a/solution.py
+++ b/solution.py
@@ -21,11 +21,12 @@
 PAIRS = TILES * DEPTH
 PIXELS = 256
 NBLK = 64
+PLANE = 8
 NVIEW = 4
 CAP = 64
 SHARE = 15
 JOINT = NVIEW * PAIRS + COPIES
-UNROLL = 4
+UNROLL = 32
 
 F32 = jnp.float32
 BF16 = jnp.bfloat16
@@ -320,10 +321,11 @@
     return jnp.where(left == upper, value, pltpu.roll(pltpu.roll(value, CAP, 1), 4, 0))
 
 
-def pack(value, chunks, wave, j):
-    folded = refold(value)
-    chunks[wave, 2 * j] = folded[0:4]
-    chunks[wave, 2 * j + 1] = folded[4:8]
+def pack(queue, chunks, wave):
+    for j in range(NBLK // 2):
+        folded = refold(queue[:, 128 * j : 128 * (j + 1)])
+        chunks[wave, 2 * j] = folded[0:4]
+        chunks[wave, 2 * j + 1] = folded[4:8]
 
 
 def unpack(chunks, wave, j):
@@ -345,8 +347,8 @@
     params, moment1, moment2, dual, z_copy, z_table, rows, owner, slot, lists, counts, target,
     table, sheet, goal, e_all, t_all, parts, gathered,
     left, masks, masked, pen_masked, onehot, source, names, place, s_value, s_first, s_second, s_dual, s_table,
-    send, got, answers, returned, z_parts, d_parts, items, item_masks, item_masked, item_hot, z_new, dual_new,
-    in_sem, out_sem, s_mine, r_mine, s_send, r_send, s_back, r_back, s_z, r_z, s_d, r_d,
+    send, got, answers, returned, z_parts, d_parts, items, queue, item_masks, item_masked, item_hot, z_new, dual_new,
+    planes_in, in_sem, out_sem, s_mine, r_mine, s_send, r_send, s_back, r_back, s_z, r_z, s_d, r_d,
 ):
     block = lax.axis_index("blocks")
     view = lax.axis_index("views")
@@ -357,23 +359,25 @@
         (moment1_in, moment1), (moment2_in, moment2), (z_table_in, z_table),
     ]
     arriving = [pltpu.make_async_copy(there, here, in_sem.at[n]) for n, (there, here) in enumerate(pairs)]
-    for copy in arriving:
+    for copy in arriving[0:4]:
         copy.start()
     barrier = pltpu.get_barrier_semaphore()
-
-    def greet(k, _):
-        pl.semaphore_signal(barrier, inc=1, device_id={"blocks": (block + k) % NBLK}, device_id_type=MESH)
-        return 0
-
-    lax.fori_loop(1, NBLK, greet, 0)
+    plane, place_in = block // PLANE, block % PLANE
+    beside = [plane * PLANE + (place_in + k) % PLANE for k in range(1, PLANE)]
+    across = [(block + PLANE * k) % NBLK for k in range(1, NBLK // PLANE)]
+    for other in beside + across:
+        pl.semaphore_signal(barrier, inc=1, device_id={"blocks": other}, device_id_type=MESH)
     for k in range(1, NVIEW):
         pl.semaphore_signal(barrier, inc=1, device_id={"views": (view + k) % NVIEW}, device_id_type=MESH)
-
     for copy in arriving[0:4]:
         copy.wait()
+    for copy in arriving[4:]:
+        copy.start()
     gathered[view] = render(cam, params, lists, counts, target, table, sheet, goal, e_all, t_all, parts)
-    pl.semaphore_wait(barrier, NBLK - 1 + NVIEW - 1)
+    pl.semaphore_wait(barrier, len(beside) + len(across) + NVIEW - 1)
     view_copies = to_views(gathered.at[view], s_mine, r_mine, view)
+    for other in across:
+        pl.semaphore_signal(planes_in, inc=1, device_id={"blocks": other}, device_id_type=MESH)
 
     for copy in arriving[4:]:
         copy.wait()
@@ -435,6 +439,7 @@
 
     for copy in view_copies:
         copy.wait()
+    pl.semaphore_wait(planes_in, len(across))
     diagonal = lax.broadcasted_iota(I32, (16, 128), 0) == lax.broadcasted_iota(I32, (16, 128), 1)
     for v in range(NVIEW):
         lanes = slice(PAIRS * v, PAIRS * (v + 1))
@@ -468,7 +473,8 @@
         for j in range(NBLK // 2):
             name = jnp.where(lane < CAP, wide(names[2 * j : 2 * j + 1, :]), wide(names[2 * j + 1 : 2 * j + 2, :]))
             found = lane_gather(blocks_of, jnp.maximum(name - 1, 0))
-            pack(jnp.where(name > 0, found, 0.0), send, wave, j)
+            queue[:, 128 * j : 128 * (j + 1)] = jnp.where(name > 0, found, 0.0)
+        pack(queue, send, wave)
         to_blocks(send, got, s_send, r_send, block, wave)
 
     high, low = split(left[...])
@@ -522,7 +528,8 @@
         z_parts[view, at, :] = fresh
         answer = groups_of(fresh, 0)
         for j in range(NBLK // 2):
-            pack(lane_gather(answer, wide(index[:, 128 * j : 128 * (j + 1)])), answers, wave, j)
+            queue[:, 128 * j : 128 * (j + 1)] = lane_gather(answer, wide(index[:, 128 * j : 128 * (j + 1)]))
+        pack(queue, answers, wave)
         to_blocks(answers, returned, s_back, r_back, block, wave)
     z_copies = to_views(z_parts.at[view], s_z, r_z, view)
 
@@ -610,8 +617,8 @@
             f32(16, COPIES), i32(NBLK, 128), i32(1, COPIES),
             f32(16, GAUSS), f32(16, GAUSS), f32(16, GAUSS), f32(16, COPIES), f32(16, ROWS),
             chunks, chunks, chunks, chunks, f32(NVIEW, 16, ROWS), f32(2, NVIEW, 8, COPIES),
-            f32(16, NBLK * CAP), bf16(64, NBLK * CAP), bf16(64, NBLK * CAP), bf16(256, NBLK * CAP), f32(NPAR, ROWS), f32(NPAR, COPIES),
-            dma((12,)), dma((5,)), dma((3,)), dma((3,)), dma((2,)), dma((2,)), dma((2,)), dma((2,)),
+            f32(16, NBLK * CAP), f32(8, NBLK * CAP), bf16(64, NBLK * CAP), bf16(64, NBLK * CAP), bf16(256, NBLK * CAP), f32(NPAR, ROWS), f32(NPAR, COPIES),
+            pltpu.SemaphoreType.REGULAR, dma((12,)), dma((5,)), dma((3,)), dma((3,)), dma((2,)), dma((2,)), dma((2,)), dma((2,)),
             dma((3,)), dma((3,)), dma((2, 3)), dma((2, 3)),
         ],
         compiler_params=pltpu.CompilerParams(

time: 48.1 us -> 45.8 us (0.952)
  Pallas kernels: 47.3 us -> 45 us
    pallas_call x1, Pallas kernels: 44.9 us -> 42.6 us  [local(): pl.pallas_call(round_kernel, out_shape=outs, in_specs=[pl.BlockSpec(memor...]
where the time goes in v3:
time: 45.8 us; the launch traced here: 45.7 us
  Pallas kernels  45 us (98%)
  between operations  0.64 us (1%)
    pallas_call x1, Pallas kernels, local(): pl.pallas_call(round_kernel, out_shape=outs, in_specs=[pl.BlockSpec(memor...  42.6 us
    pallas_call x1, Pallas kernels, local(): pl.pallas_call(finish_kernel, out_shape=outs, in_specs=[anywhere()] * 5,...  2.4 us

profile of v3, /device:TPU:1, one launch (start us, length us, event | category | flops | bytes accessed | tf_op | source)
XLA Modules:
  0.0 45.7 jit_solution(12501555913693340801)
XLA Ops:
  0.6 42.6 %round.1 = (f32[59,2048]{1,0:T(8,128)}, f32[59,2048]{1,0:T(8,128)}, f32[59,2048]{1,0:T(8,128)}, f32[59,1024]{1,0:T(8,128)}, f32[59,1024]{1,0:T(8,128)}) custom-call(f32[1,24]{1,0:T(1,128)} %cam.1, f32[59,2048]{1,0:T(8,128)} %params_in.1, f32[59,2048]{1,0:T(8,128)} %moment1_in.1, f32[59,2048]{1,0:T(8,128)} %moment2_in.1, f32[59,1024]{1,0:T(8,128)} %dual_in.1, ...), custom_call_target="tpu_custom_call" | custom-call | tf_op jit(solution)/shard_map/round/pallas_call | solution.py:605
  43.3 2.4 %finish.1 = (f32[59,2048]{1,0:T(8,128)}, f32[59,2048]{1,0:T(8,128)}, f32[59,2048]{1,0:T(8,128)}, f32[59,1024]{1,0:T(8,128)}, f32[59,1024]{1,0:T(8,128)}) custom-call(f32[59,2048]{1,0:T(8,128)} %get-tuple-element.10.refs_0_, f32[59,2048]{1,0:T(8,128)} %get-tuple-element.11.refs_1_, f32[59,2048]{1,0:T(8,128)} %get-tuple-element.12.refs_2_, ...), custom_call_target="tpu_custom_call" | custom-call | tf_op jit(solution)/shard_map/finish/pallas_call | solution.py:633

commit v4 on v3

--- a/solution.py
+++ b/solution.py
@@ -477,29 +477,33 @@
         pack(queue, send, wave)
         to_blocks(send, got, s_send, r_send, block, wave)
 
-    high, low = split(left[...])
-    for h in range(8):
-        mask = masks[16 * h : 16 * h + 16, :]
+    leaving = []
+
+    def step_half(half):
+        high, low = split(left[...])
         for n in range(4):
-            masked[128 * h + 16 * n : 128 * h + 16 * n + 16, :] = high[16 * n : 16 * n + 16, :] * mask
-            masked[128 * h + 64 + 16 * n : 128 * h + 80 + 16 * n, :] = low[16 * n : 16 * n + 16, :] * mask
-    total = lax.dot_general(masked[...], onehot[...], NT, preferred_element_type=F32)
-    for h in range(8):
-        both = total[128 * h : 128 * h + 64, :] + total[128 * h + 64 : 128 * h + 128, :]
-        lanes = slice(256 * h, 256 * (h + 1))
-        value = params[:, lanes]
-        grad = both[0:NPAR] + both[NPAR : NPAR + 1] * value
-        params[:, lanes], moment1[:, lanes], moment2[:, lanes] = adam(
-            value, moment1[:, lanes], moment2[:, lanes], grad
-        )
-    leaving = [
-        pltpu.make_async_copy(here, there, out_sem.at[n])
-        for n, (here, there) in enumerate(
-            [(params, params_out), (moment1, moment1_out), (moment2, moment2_out), (z_new, z_out), (dual_new, dual_out)]
-        )
-    ]
-    for copy in leaving[0:3]:
-        copy.start()
+            mask = masks[64 * half + 16 * n : 64 * half + 16 * n + 16, :]
+            for part in range(4):
+                rows_at = slice(16 * part, 16 * part + 16)
+                masked[128 * n + 16 * part : 128 * n + 16 * part + 16, :] = high[rows_at, :] * mask
+                masked[128 * n + 64 + 16 * part : 128 * n + 80 + 16 * part, :] = low[rows_at, :] * mask
+        total = lax.dot_general(masked[...], onehot[...], NT, preferred_element_type=F32)
+        for n in range(4):
+            both = total[128 * n : 128 * n + 64, :] + total[128 * n + 64 : 128 * n + 128, :]
+            lanes = slice(1024 * half + 256 * n, 1024 * half + 256 * (n + 1))
+            value = params[:, lanes]
+            grad = both[0:NPAR] + both[NPAR : NPAR + 1] * value
+            params[:, lanes], moment1[:, lanes], moment2[:, lanes] = adam(
+                value, moment1[:, lanes], moment2[:, lanes], grad
+            )
+        lanes = pl.ds(1024 * half, 1024)
+        for n, (here, there) in enumerate([(params, params_out), (moment1, moment1_out), (moment2, moment2_out)]):
+            copy = pltpu.make_async_copy(here.at[:, lanes], there.at[:, lanes], out_sem.at[3 * half + n])
+            copy.start()
+            leaving.append(copy)
+
+    step_half(0)
+
     last = lax.broadcasted_iota(I32, (8, NBLK * CAP), 0) == 7
     for wave in range(2):
         at = slice(8 * wave, 8 * wave + 8)
@@ -510,18 +514,18 @@
         if wave == 0:
             label = items[7:8, :].astype(I32)
             index = jnp.maximum(label - 1, 0)
-            group = jnp.broadcast_to(jnp.where(label > 0, index >> 8, 4), (16, NBLK * CAP))
-            for h in range(4):
+            group = jnp.broadcast_to(jnp.where(label > 0, index >> 7, 8), (16, NBLK * CAP))
+            for h in range(8):
                 item_masks[16 * h : 16 * h + 16, :] = jnp.where(group == h, 1.0, 0.0).astype(BF16)
-            hot = lax.broadcasted_iota(I32, (256, NBLK * CAP), 0) == (index & 255)
+            hot = lax.broadcasted_iota(I32, (128, NBLK * CAP), 0) == (index & 127)
             item_hot[...] = jnp.where(hot, 1.0, 0.0).astype(BF16)
             value = jnp.where(last, 1.0, value)
         high = value.astype(BF16).astype(F32)
         both = jnp.concatenate([high, value - high], axis=0).astype(BF16)
-        for h in range(4):
+        for h in range(8):
             item_masked[16 * h : 16 * h + 16, :] = both * item_masks[16 * h : 16 * h + 16, :]
         total = lax.dot_general(item_masked[...], item_hot[...], NT, preferred_element_type=F32)
-        total = jnp.concatenate([total[16 * h : 16 * h + 8, :] + total[16 * h + 8 : 16 * h + 16, :] for h in range(4)], axis=1)
+        total = jnp.concatenate([total[16 * h : 16 * h + 8, :] + total[16 * h + 8 : 16 * h + 16, :] for h in range(8)], axis=1)
         if wave == 0:
             number = 1.0 + total[7:8, :]
         fresh = (s_table[at, :] + total) / number
@@ -532,6 +536,7 @@
         pack(queue, answers, wave)
         to_blocks(answers, returned, s_back, r_back, block, wave)
     z_copies = to_views(z_parts.at[view], s_z, r_z, view)
+    step_half(1)
 
     d_copies = []
     for wave in range(2):
@@ -547,13 +552,15 @@
             for v in range(NVIEW):
                 for part in range(2):
                     assemble(z_new, z_parts.at[v, 8 * part : 8 * part + 8], v, part)
-            leaving[3].start()
+            leaving.append(pltpu.make_async_copy(z_new, z_out, out_sem.at[6]))
+            leaving[-1].start()
     for wave in range(2):
         for copy in d_copies[wave]:
             copy.wait()
         for v in range(NVIEW):
             assemble(dual_new, d_parts.at[wave, v], v, wave)
-    leaving[4].start()
+    leaving.append(pltpu.make_async_copy(dual_new, dual_out, out_sem.at[7]))
+    leaving[-1].start()
     for copy in leaving:
         copy.wait()
 
@@ -613,12 +620,12 @@
             i32(1, COPIES), i32(1, COPIES), i32(1, COPIES), i32(TILES, DEPTH), i32(1, TILES), f32(3, TILES * PIXELS),
             f32(16, GAUSS), f32(PAIRS, 16), f32(48, PIXELS), f32(PAIRS, PIXELS), f32(PAIRS, PIXELS),
             bf16(10, PAIRS, PIXELS), f32(NVIEW, 16, PAIRS),
-            f32(64, JOINT), bf16(128, JOINT), bf16(1024, JOINT), bf16(256, COPIES), bf16(256, JOINT),
+            f32(64, JOINT), bf16(128, JOINT), bf16(512, JOINT), bf16(256, COPIES), bf16(256, JOINT),
             f32(16, COPIES), i32(NBLK, 128), i32(1, COPIES),
             f32(16, GAUSS), f32(16, GAUSS), f32(16, GAUSS), f32(16, COPIES), f32(16, ROWS),
             chunks, chunks, chunks, chunks, f32(NVIEW, 16, ROWS), f32(2, NVIEW, 8, COPIES),
-            f32(16, NBLK * CAP), f32(8, NBLK * CAP), bf16(64, NBLK * CAP), bf16(64, NBLK * CAP), bf16(256, NBLK * CAP), f32(NPAR, ROWS), f32(NPAR, COPIES),
-            pltpu.SemaphoreType.REGULAR, dma((12,)), dma((5,)), dma((3,)), dma((3,)), dma((2,)), dma((2,)), dma((2,)), dma((2,)),
+            f32(16, NBLK * CAP), f32(8, NBLK * CAP), bf16(128, NBLK * CAP), bf16(128, NBLK * CAP), bf16(128, NBLK * CAP), f32(NPAR, ROWS), f32(NPAR, COPIES),
+            pltpu.SemaphoreType.REGULAR, dma((12,)), dma((8,)), dma((3,)), dma((3,)), dma((2,)), dma((2,)), dma((2,)), dma((2,)),
             dma((3,)), dma((3,)), dma((2, 3)), dma((2, 3)),
         ],
         compiler_params=pltpu.CompilerParams(

time: 45.8 us -> 45.2 us (0.987)
  Pallas kernels: 45 us -> 44.4 us
    pallas_call x1, Pallas kernels: 42.6 us -> 42 us  [local(): pl.pallas_call(round_kernel, out_shape=outs, in_specs=[pl.BlockSpec(memor...]
where the time goes in v4:
time: 45.2 us; the launch traced here: 45.1 us
  Pallas kernels  44.4 us (98%)
  between operations  0.64 us (1%)
    pallas_call x1, Pallas kernels, local(): pl.pallas_call(round_kernel, out_shape=outs, in_specs=[pl.BlockSpec(memor...  42 us
    pallas_call x1, Pallas kernels, local(): pl.pallas_call(finish_kernel, out_shape=outs, in_specs=[anywhere()] * 5,...  2.4 us

profile of v4, /device:TPU:1, one launch (start us, length us, event | category | flops | bytes accessed | tf_op | source)
XLA Modules:
  0.0 45.1 jit_solution(7277872491381421914)
XLA Ops:
  0.6 42.0 %round.1 = (f32[59,2048]{1,0:T(8,128)}, f32[59,2048]{1,0:T(8,128)}, f32[59,2048]{1,0:T(8,128)}, f32[59,1024]{1,0:T(8,128)}, f32[59,1024]{1,0:T(8,128)}) custom-call(f32[1,24]{1,0:T(1,128)} %cam.1, f32[59,2048]{1,0:T(8,128)} %params_in.1, f32[59,2048]{1,0:T(8,128)} %moment1_in.1, f32[59,2048]{1,0:T(8,128)} %moment2_in.1, f32[59,1024]{1,0:T(8,128)} %dual_in.1, ...), custom_call_target="tpu_custom_call" | custom-call | tf_op jit(solution)/shard_map/round/pallas_call | solution.py:612
  42.7 2.4 %finish.1 = (f32[59,2048]{1,0:T(8,128)}, f32[59,2048]{1,0:T(8,128)}, f32[59,2048]{1,0:T(8,128)}, f32[59,1024]{1,0:T(8,128)}, f32[59,1024]{1,0:T(8,128)}) custom-call(f32[59,2048]{1,0:T(8,128)} %get-tuple-element.10.refs_0_, f32[59,2048]{1,0:T(8,128)} %get-tuple-element.11.refs_1_, f32[59,2048]{1,0:T(8,128)} %get-tuple-element.12.refs_2_, ...), custom_call_target="tpu_custom_call" | custom-call | tf_op jit(solution)/shard_map/finish/pallas_call | solution.py:640

commit v5 on v4

--- a/solution.py
+++ b/solution.py
@@ -299,12 +299,12 @@
     whole.wait_recv()
 
 
-def to_views(piece, send_sem, recv_sem, view):
+def to_views(piece, send_sem, recv_sem, view, there=None):
     copies = []
     for k in range(1, NVIEW):
         copy = pltpu.make_async_remote_copy(
             src_ref=piece,
-            dst_ref=piece,
+            dst_ref=piece if there is None else there,
             send_sem=send_sem.at[k - 1],
             recv_sem=recv_sem.at[k - 1],
             device_id={"views": (view + k) % NVIEW},
@@ -343,11 +343,11 @@
 def round_kernel(
     cam, params_in, moment1_in, moment2_in, dual_in, z_copy_in, z_table_in, rows_in, owner_in, slot_in,
     lists_in, counts_in, target_in,
-    params_out, moment1_out, moment2_out, z_out, dual_out,
+    params_out, moment1_out, moment2_out, z_out, d_out,
     params, moment1, moment2, dual, z_copy, z_table, rows, owner, slot, lists, counts, target,
     table, sheet, goal, e_all, t_all, parts, gathered,
     left, masks, masked, pen_masked, onehot, source, names, place, s_value, s_first, s_second, s_dual, s_table,
-    send, got, answers, returned, z_parts, d_parts, items, queue, item_masks, item_masked, item_hot, z_new, dual_new,
+    send, got, answers, returned, z_parts, d_own, items, queue, item_masks, item_masked, item_hot, z_new,
     planes_in, in_sem, out_sem, s_mine, r_mine, s_send, r_send, s_back, r_back, s_z, r_z, s_d, r_d,
 ):
     block = lax.axis_index("blocks")
@@ -544,8 +544,10 @@
         wait_blocks(answers, returned, s_back, r_back, block, wave)
         for j in range(NBLK // 2):
             items[at, 128 * j : 128 * (j + 1)] = unpack(returned, wave, j)
-        d_parts[wave, view] = source[at, :] - fetch(items, 8 * wave, place)
-        d_copies.append(to_views(d_parts.at[wave, view], s_d.at[wave], r_d.at[wave], view))
+        d_own[wave] = source[at, :] - fetch(items, 8 * wave, place)
+        d_copies += to_views(d_own.at[wave], s_d.at[wave], r_d.at[wave], view, d_out.at[wave, view])
+        leaving.append(pltpu.make_async_copy(d_own.at[wave], d_out.at[wave, view], out_sem.at[7 + wave]))
+        leaving[-1].start()
         if wave == 0:
             for copy in z_copies:
                 copy.wait()
@@ -554,21 +556,18 @@
                     assemble(z_new, z_parts.at[v, 8 * part : 8 * part + 8], v, part)
             leaving.append(pltpu.make_async_copy(z_new, z_out, out_sem.at[6]))
             leaving[-1].start()
-    for wave in range(2):
-        for copy in d_copies[wave]:
-            copy.wait()
-        for v in range(NVIEW):
-            assemble(dual_new, d_parts.at[wave, v], v, wave)
-    leaving.append(pltpu.make_async_copy(dual_new, dual_out, out_sem.at[7]))
-    leaving[-1].start()
+    for copy in d_copies:
+        copy.wait()
     for copy in leaving:
         copy.wait()
 
 
 def finish_kernel(*refs):
-    sources, targets, staged, in_sem, out_sem = refs[0:5], refs[5:10], refs[10:15], refs[15], refs[16]
+    sources, targets, staged, dual_new, in_sem, out_sem = refs[0:5], refs[5:10], refs[10:15], refs[15], refs[16], refs[17]
+    parts = pltpu.make_async_copy(sources[4], staged[4], in_sem.at[7])
+    duals = pltpu.make_async_copy(dual_new, targets[4], out_sem.at[7])
     steps = []
-    for n, ref in enumerate(sources):
+    for n, ref in enumerate(sources[0:4]):
         for piece in range(ref.shape[1] // ROWS):
             lanes = pl.ds(ROWS * piece, ROWS)
             at = len(steps)
@@ -578,13 +577,21 @@
                     pltpu.make_async_copy(staged[n].at[:, lanes], targets[n].at[:, lanes], out_sem.at[at]),
                 )
             )
+    parts.start()
     for arrive, _ in steps:
         arrive.start()
-    for arrive, leave in steps:
+    for n, (arrive, leave) in enumerate(steps):
         arrive.wait()
         leave.start()
+        if n == 2:
+            parts.wait()
+            for v in range(NVIEW):
+                for wave in range(2):
+                    assemble(dual_new, staged[4].at[wave, v], v, wave)
+            duals.start()
     for _, leave in steps:
         leave.wait()
+    duals.wait()
 
 
 def anywhere():
@@ -607,11 +614,12 @@
     def i32(*dims):
         return pltpu.VMEM(dims, I32)
 
+    parts = shape((2, NVIEW, 8, COPIES), F32)
     chunks = f32(2, NBLK, 4, 128)
     dma = pltpu.SemaphoreType.DMA
     results = pl.pallas_call(
         round_kernel,
-        out_shape=outs,
+        out_shape=(*outs[0:4], parts),
         in_specs=[pl.BlockSpec(memory_space=pltpu.SMEM)] + [anywhere()] * 12,
         out_specs=(anywhere(),) * 5,
         scratch_shapes=[
@@ -623,9 +631,9 @@
             f32(64, JOINT), bf16(128, JOINT), bf16(512, JOINT), bf16(256, COPIES), bf16(256, JOINT),
             f32(16, COPIES), i32(NBLK, 128), i32(1, COPIES),
             f32(16, GAUSS), f32(16, GAUSS), f32(16, GAUSS), f32(16, COPIES), f32(16, ROWS),
-            chunks, chunks, chunks, chunks, f32(NVIEW, 16, ROWS), f32(2, NVIEW, 8, COPIES),
-            f32(16, NBLK * CAP), f32(8, NBLK * CAP), bf16(128, NBLK * CAP), bf16(128, NBLK * CAP), bf16(128, NBLK * CAP), f32(NPAR, ROWS), f32(NPAR, COPIES),
-            pltpu.SemaphoreType.REGULAR, dma((12,)), dma((8,)), dma((3,)), dma((3,)), dma((2,)), dma((2,)), dma((2,)), dma((2,)),
+            chunks, chunks, chunks, chunks, f32(NVIEW, 16, ROWS), f32(2, 8, COPIES),
+            f32(16, NBLK * CAP), f32(8, NBLK * CAP), bf16(128, NBLK * CAP), bf16(128, NBLK * CAP), bf16(128, NBLK * CAP), f32(NPAR, ROWS),
+            pltpu.SemaphoreType.REGULAR, dma((12,)), dma((9,)), dma((3,)), dma((3,)), dma((2,)), dma((2,)), dma((2,)), dma((2,)),
             dma((3,)), dma((3,)), dma((2, 3)), dma((2, 3)),
         ],
         compiler_params=pltpu.CompilerParams(
@@ -642,7 +650,7 @@
         out_shape=outs,
         in_specs=[anywhere()] * 5,
         out_specs=(anywhere(),) * 5,
-        scratch_shapes=[f32(*out.shape) for out in outs] + [dma((8,)), dma((8,))],
+        scratch_shapes=[f32(*out.shape) for out in (*outs[0:4], parts, outs[4])] + [dma((8,)), dma((8,))],
         compiler_params=pltpu.CompilerParams(vmem_limit_bytes=56 * 1024 * 1024),
         name="finish",
     )(*results)

time: 45.2 us -> 44.7 us (0.989)
  Pallas kernels: 44.4 us -> 43.9 us
    pallas_call x1, Pallas kernels: 42 us -> 41.5 us  [local(): pl.pallas_call(round_kernel, out_shape=(*outs[0:4], parts), in_specs=[pl....]
where the time goes in v5:
time: 44.7 us; the launch traced here: 44.6 us
  Pallas kernels  43.9 us (98%)
  between operations  0.64 us (1%)
    pallas_call x1, Pallas kernels, local(): pl.pallas_call(round_kernel, out_shape=(*outs[0:4], parts), in_specs=[pl....  41.5 us
    pallas_call x1, Pallas kernels, local(): pl.pallas_call(finish_kernel, out_shape=outs, in_specs=[anywhere()] * 5,...  2.48 us

profile of v5, /device:TPU:1, one launch (start us, length us, event | category | flops | bytes accessed | tf_op | source)
XLA Modules:
  0.0 44.6 jit_solution(8365440547759420558)
XLA Ops:
  0.6 41.5 %round.1 = (f32[59,2048]{1,0:T(8,128)}, f32[59,2048]{1,0:T(8,128)}, f32[59,2048]{1,0:T(8,128)}, f32[59,1024]{1,0:T(8,128)}, f32[2,4,8,1024]{3,2,1,0:T(8,128)}) custom-call(f32[1,24]{1,0:T(1,128)} %cam.1, f32[59,2048]{1,0:T(8,128)} %params_in.1, f32[59,2048]{1,0:T(8,128)} %moment1_in.1, f32[59,2048]{1,0:T(8,128)} %moment2_in.1, f32[59,1024]{1,0:T(8,128)} %dual_in.1, ...), custom_call_target="tpu_custom_call" | custom-call | tf_op jit(solution)/shard_map/round/pallas_call | solution.py:620
  42.1 2.5 %finish.1 = (f32[59,2048]{1,0:T(8,128)}, f32[59,2048]{1,0:T(8,128)}, f32[59,2048]{1,0:T(8,128)}, f32[59,1024]{1,0:T(8,128)}, f32[59,1024]{1,0:T(8,128)}) custom-call(f32[59,2048]{1,0:T(8,128)} %get-tuple-element.10.refs_0_, f32[59,2048]{1,0:T(8,128)} %get-tuple-element.11.refs_1_, f32[59,2048]{1,0:T(8,128)} %get-tuple-element.12.refs_2_, ...), custom_call_target="tpu_custom_call" | custom-call | tf_op jit(solution)/shard_map/finish/pallas_call | solution.py:648
